TPU v7x, 256 devices: a whole 4x4x8 slice. The times are simulated.
256 devices in a mesh: dp: 2 (over x_lo), row: 8 (over x_hi, y), col: 16 (over z, core).
Axes of the slice: x: 4 (x_hi: 2, x_lo: 2; x = x_hi * 2 + x_lo), y: 4, z: 8, core: 2. Of those that a mesh axis runs over, the one named last changes fastest.
Arguments:
- tokens: bfloat16 [32768, 1024], P(('dp', 'row', 'col')), may hold values from -6 to 6
- out_grad: bfloat16 [32768, 1024], P(('dp', 'row', 'col')), may hold values from -3 to 3
- w_up: bfloat16 [1024, 4096], P('row', 'col'), may hold values from -0.1875 to 0.1875
- w_down: bfloat16 [4096, 1024], P('col', 'row'), may hold values from -0.09375 to 0.09375
Outputs:
- tokens_grad: bfloat16 [32768, 1024], P(('dp', 'row', 'col'))
- up_grad: bfloat16 [1024, 4096], P('row', 'col')
- down_grad: bfloat16 [4096, 1024], P('col', 'row')
All inputs are finite; a program needn't handle non-finite values.
Results may differ from a plain program's by a relative error of at most 0.0049.
Values may be sent and summed in bfloat16 or wider, within the bound.
A program may use at most 64 MiB of HBM per device.

v0:
```python
import jax
import jax.numpy as jnp
from jax import lax
from jax.sharding import PartitionSpec as P


def gelu_tanh(value):
    return jax.nn.gelu(value, approximate=True)


def gelu_back(pre, hid_grad):
    hidden_f, pullback = jax.vjp(gelu_tanh, pre)
    (pre_grad_f,) = pullback(hid_grad)
    return (hidden_f.astype(jnp.bfloat16), pre_grad_f.astype(jnp.bfloat16))


def inner_rows(left, right):
    return lax.dot_general(
        left, right, (((0,), (0,)), ((), ())), preferred_element_type=jnp.float32
    )


def inner_cols(left, right):
    return lax.dot_general(
        left, right, (((1,), (1,)), ((), ())), preferred_element_type=jnp.float32
    )


def shards(tokens, out_grad, w_up, w_down):
    rows_x, rows_dy = (
        lax.all_gather(tokens, "col", axis=0, tiled=True),
        lax.all_gather(out_grad, "col", axis=0, tiled=True),
    )
    up_full, down_full = (
        lax.all_gather(w_up, "row", axis=0, tiled=True),
        lax.all_gather(w_down.T, "row", axis=0, tiled=True),
    )
    pre = jnp.dot(rows_x, up_full, preferred_element_type=jnp.float32)
    hid_grad = jnp.dot(rows_dy, down_full, preferred_element_type=jnp.float32)
    hidden, pre_grad = gelu_back(pre, hid_grad)
    units = w_up.shape[1]
    whole = lax.psum(
        jnp.concatenate([inner_rows(rows_x, pre_grad), inner_rows(rows_dy, hidden)], axis=1), "dp"
    )
    totals = lax.psum_scatter(whole, "row", scatter_dimension=0, tiled=True)
    up_grad = totals[:, :units].astype(jnp.bfloat16)
    down_grad = totals[:, units:].T.astype(jnp.bfloat16)
    tokens_grad = lax.psum_scatter(
        inner_cols(pre_grad, up_full), "col", scatter_dimension=0, tiled=True
    )
    return (tokens_grad.astype(jnp.bfloat16), up_grad, down_grad)


def solution(mesh):
    return jax.shard_map(
        shards,
        mesh=mesh,
        in_specs=(
            P(("dp", "row", "col"), None),
            P(("dp", "row", "col"), None),
            P("row", "col"),
            P("col", "row"),
        ),
        out_specs=(P(("dp", "row", "col"), None), P("row", "col"), P("col", "row")),
        check_vma=False,
    )
```

profile of v0, /device:TPU:2, one launch (start us, length us, event | category | flops | bytes accessed | tf_op | source)
XLA Modules:
  0.0 266.9 jit_solution(13403392269823120237)
XLA Ops:
  7.2 0.0 all-gather.3.cloned.1.call-start
  7.2 0.7 all-gather.3.cloned.1.call-update
  7.9 0.0 all-gather.5.cloned.1.call-start
  7.9 0.7 all-gather.5.cloned.1.call-update
  8.6 0.0 reduce-scatter.5.cloned.1.call-start
  8.7 35.3 %all_gather.15 = bf16[1024,256]{1,0:T(8,128)(2,1)S(1)} all-gather(bf16[128,256]{1,0:T(8,128)(2,1)} %param.6), channel_id=1, replica_groups=mesh['dp'=2,'row'=8,'col'=16] {'row'}, dimensions={0}, use_global_device_ids=true | all-gather | bytes 589824 | tf_op jit(solution)/shard_map/all_gather | solution.py:35
  44.0 30.9 %all_gather.13 = bf16[1024,256]{0,1:T(8,128)(2,1)S(1)} all-gather(bf16[128,256]{0,1:T(8,128)(2,1)} %bitcast.16), channel_id=1, replica_groups=mesh['dp'=2,'row'=8,'col'=16] {'row'}, dimensions={0}, use_global_device_ids=true | all-gather | bytes 589824 | tf_op jit(solution)/shard_map/all_gather | solution.py:36
  74.9 0.0 all-gather.3.cloned.1.call-done
  74.9 4.9 %fusion.15 = f32[2048,256]{1,0:T(8,128)} fusion(bf16[2048,1024]{1,0:T(8,128)(2,1)} %all-gather.3.cloned.1.call-done, bf16[1024,256]{0,1:T(8,128)(2,1)S(1)} %all_gather.13), kind=kOutput, calls=%fused_computation.22 | convolution fusion | flops 1073741824 | bytes 6815744 | tf_op jit(solution)/shard_map/dot_general | solution.py:39
  79.8 17.7 %all-gather.5.cloned.1.call-done = bf16[2048,1024]{1,0:T(8,128)(2,1)} async-done(((bf16[128,1024]{1,0:T(8,128)(2,1)}), bf16[2048,1024]{1,0:T(8,128)(2,1)}) %all-gather.5.cloned.1.call-update) | async-done | bytes 4194320 | tf_op jit(solution)/shard_map/all_gather | solution.py:31
  97.5 0.0 copy-start.1
  97.5 5.3 %fusion.6 = (bf16[2048,256]{1,0:T(8,128)(2,1)S(1)}, f32[2048,256]{1,0:T(8,128)S(1)}) fusion(f32[2048,256]{1,0:T(8,128)} %fusion.15, bf16[2048,1024]{1,0:T(8,128)(2,1)} %all-gather.5.cloned.1.call-done, bf16[1024,256]{1,0:T(8,128)(2,1)S(1)} %all_gather.15), kind=kOutput, calls=%fused_computation.8 | convolution fusion | flops 1084227584 | bytes 9961472 | tf_op jit(solution)/shard_map/dot_general | solution.py:38
  102.8 0.0 copy-done.1
  102.8 0.0 copy-start
  102.8 1.3 convolution_bitcast_fusion.1
  104.1 0.9 copy-done
  105.0 1.5 convolution_bitcast_fusion
  106.5 1.5 pad_maximum_fusion
  108.0 0.0 reduce-scatter.5.cloned.1.call-update
  108.0 0.0 reduce-scatter.3.cloned.1.call-start
  108.1 4.5 %fusion.16 = f32[2048,1024]{1,0:T(8,128)} fusion(bf16[2048,256]{1,0:T(8,128)(2,1)S(1)} %get-tuple-element.8, bf16[1024,256]{1,0:T(8,128)(2,1)S(1)} %all_gather.15), kind=kOutput, calls=%fused_computation.23 | convolution fusion | flops 1073741824 | bytes 9961472 | tf_op jit(solution)/shard_map/dot_general | solution.py:24
  112.6 0.0 reduce-scatter.3.cloned.1.call-update
  112.6 73.2 %reduce-scatter.5.cloned.1.call-done = f32[128,512]{0,1:T(8,128)} async-done(((f32[1024,512]{0,1:T(8,128)}), f32[128,512]{0,1:T(8,128)}) %reduce-scatter.5.cloned.1.call-update) | async-done | bytes 262160 | tf_op jit(solution)/shard_map/reduce_scatter | solution.py:45
  185.9 13.3 %all-reduce.1 = bf16[128,512]{0,1:T(8,128)(2,1)S(1)} all-reduce(f32[128,512]{0,1:T(8,128)} %reduce-scatter.5.cloned.1.call-done), channel_id=1, replica_groups=mesh['dp'=2,'row'=8,'col'=16] {'dp'}, use_global_device_ids=true, to_apply=%region_1.0 | all-reduce | flops 65536 | bytes 393216 | tf_op jit(solution)/shard_map/psum | solution.py:42
  199.2 0.6 slice_bitcast_fusion
  199.8 0.7 copy.7
  200.5 58.1 %reduce-scatter.3.cloned.1.call-done = f32[128,1024]{1,0:T(8,128)} async-done(((f32[2048,1024]{1,0:T(8,128)}), f32[128,1024]{1,0:T(8,128)}) %reduce-scatter.3.cloned.1.call-update) | async-done | bytes 524304 | tf_op jit(solution)/shard_map/reduce_scatter | solution.py:48
  258.6 1.8 convert_element_type.15
Async XLA Ops:
  7.2 67.7 %all-gather.3.cloned.1.call-start = ((), (), s32[]{:S(2)}) async-start(), calls=%async_computation.2 | async-start | bytes 4456448 | tf_op jit(solution)/shard_map/all_gather | solution.py:32
  7.9 89.6 %all-gather.5.cloned.1.call-start = ((), (), s32[]{:S(2)}) async-start(), calls=%async_computation.3 | async-start | bytes 4456448 | tf_op jit(solution)/shard_map/all_gather | solution.py:31
  8.6 177.2 %reduce-scatter.5.cloned.1.call-start = ((), (), s32[]{:S(2)}) async-start(), calls=%async_computation.5 | async-start | bytes 2359296 | tf_op jit(solution)/shard_map/reduce_scatter | solution.py:45
  97.5 5.4 %copy-start.1 = (bf16[2048,1024]{1,0:T(8,128)(2,1)S(1)}, bf16[2048,1024]{1,0:T(8,128)(2,1)}, u32[]{:S(2)}) copy-start(bf16[2048,1024]{1,0:T(8,128)(2,1)} %all-gather.5.cloned.1.call-done) | copy-start | bytes 12582916
  102.8 2.2 copy-start
  108.0 150.6 %reduce-scatter.3.cloned.1.call-start = ((), (), s32[]{:S(2)}) async-start(), calls=%async_computation.4 | async-start | bytes 8912896 | tf_op jit(solution)/shard_map/reduce_scatter | solution.py:48
Sparse Core Ops, SparseCore 0:
  9.8 45.0 all-gather.2
  56.7 40.6 all-gather.4
  108.1 77.6 reduce-scatter.4
  188.3 70.2 reduce-scatter.2
where the time goes:
time: 267 us
  waiting for transfers between devices  150 us (56%)
  blocking collectives  79.5 us (30%)
  matrix products  17.6 us (7%)
  between operations  13.8 us (5%)
  other arithmetic  3.27 us (1%)
    reduce_scatter x1, waiting for transfers between devices, shards(): totals = lax.psum_scatter(whole, 'row', scatter_dimension=0, tiled=True)  73.2 us
    reduce_scatter x1, waiting for transfers between devices, shards(): lax.psum_scatter(inner_cols(pre_grad, up_full), 'col', scatter_dimension=...  58.1 us
    all_gather x1, blocking collectives, shards(): lax.all_gather(w_up, 'row', axis=0, tiled=True)  35.3 us
    all_gather x1, blocking collectives, shards(): lax.all_gather(w_down.T, 'row', axis=0, tiled=True)  30.9 us
    all_gather x1, waiting for transfers between devices, shards(): lax.all_gather(tokens, 'col', axis=0, tiled=True)  17.7 us
    psum x1, blocking collectives, shards(): lax.psum(jnp.concatenate([inner_rows(rows_x, pre_grad), inner_rows(rows_d...  13.3 us
    dot_general x1, matrix products, shards(): pre = jnp.dot(rows_x, up_full, preferred_element_type=jnp.float32)  5.34 us
  transfers between devices with their start and end apart: 4, of which 3 were waited for; matrix products, arithmetic and copies ran while one was open for 4% of the time, Pallas kernels for 0%

commit v1 on v0

v1 whole, which is shorter than its diff:
```python
import functools

import jax
import jax.numpy as jnp
from jax import lax
from jax.experimental import pallas as pl
from jax.experimental.pallas import tpu as pltpu
from jax.sharding import PartitionSpec as P

MESH = pl.DeviceIdType.MESH
BF16 = jnp.bfloat16
F32 = jnp.float32
NX, NY, NZ = 4, 4, 8


def gelu_pair(pre, hid_grad):
    k = 0.7978845608028654
    sq = pre * pre
    t = jnp.tanh(pre * (k + (k * 0.044715) * sq))
    half = 0.5 * (1.0 + t)
    hidden = pre * half
    slope = half + (0.5 * pre) * (1.0 - t * t) * (k + (3.0 * k * 0.044715) * sq)
    return hidden.astype(BF16), (hid_grad * slope).astype(BF16)


def kernel(
    tok, dy, wu, wd, dx_o, gu_o, gd_o,
    TOK, DY, W, WM, PG, HID, DWS, RX, SX, RZ, FS, FIN, DXS, DXC, DXY,
    ls, tks, tkr, dys, dyr, cts, ctr, cds, cdr, s1s, s1r, s2s, s2r, s3s, s3r, s3hs, s3hr,
    rxs, rxr, rzs, rzr, fs, fr, dcs, dcr, dvs, dvr,
):
    a = lax.axis_index("dp")
    row = lax.axis_index("row")
    col = lax.axis_index("col")
    xh, y = row // NY, row % NY
    z, c = col // 2, col % 2
    x = xh * 2 + a
    xr = [x, (x + 1) % NX, (x + 2) % NX, (x + 3) % NX]
    yr = [y, (y + 1) % NY, (y + 2) % NY, (y + 3) % NY]
    zr = [(z + k) % NZ for k in range(NZ)]

    def dev(x_, y_, z_, c_):
        return (x_ % 2, (x_ // 2) * NY + y_, z_ * 2 + c_)

    def send(src, dst, ss, rs, to):
        cp = pltpu.make_async_remote_copy(
            src_ref=src, dst_ref=dst, send_sem=ss, recv_sem=rs, device_id=to, device_id_type=MESH
        )
        cp.start()
        pending.append(cp)

    def arrived(ref, rs):
        pltpu.make_async_remote_copy(
            src_ref=ref, dst_ref=ref, send_sem=rs, recv_sem=rs, device_id=mate, device_id_type=MESH
        ).wait_recv()

    pending = []
    mate = dev(x, y, z, 1 - c)
    xo = xh * 2 + 1 - a
    peers = (
        [mate]
        + [dev(x, yr[k], z, c) for k in (1, 2, 3)]
        + [dev(xr[k], y, z, c) for k in (1, 2, 3)]
        + [dev(x, y, zr[k], c) for k in range(1, NZ)]
        + [dev(xo, yr[k], z, c) for k in (1, 2, 3)]
    )
    barrier = pltpu.get_barrier_semaphore()
    for p in peers:
        pl.semaphore_signal(barrier, inc=1, device_id=p, device_id_type=MESH)
    pl.semaphore_wait(barrier, len(peers))

    def block(ref, y_, c_):
        return ref.at[pl.ds(pl.multiple_of((c_ * NY + y_) * 128, 128), 128)]

    yp, ym = dev(x, yr[1], z, c), dev(x, yr[3], z, c)
    xp, xm = dev(xr[1], y, z, c), dev(xr[3], y, z, c)

    send(tok, block(TOK, y, c), tks.at[0], tkr.at[y], yp)
    send(dy, block(DY, y, c), dys.at[0], dyr.at[y], ym)
    send(dy, block(DY, y, c), dys.at[1], dyr.at[y], yp)
    send(tok, block(TOK, y, c), tks.at[1], tkr.at[y], ym)
    send(tok, block(TOK, y, c), cts.at[0], ctr.at[y], mate)
    send(dy, block(DY, y, c), cds.at[0], cdr.at[y], mate)
    own = [
        pltpu.make_async_copy(tok, block(TOK, y, c), ls.at[0]),
        pltpu.make_async_copy(dy, block(DY, y, c), ls.at[1]),
    ]
    for cp in own:
        cp.start()

    @pl.when(a == 0)
    def _():
        WM[...] = wu[...].T

    @pl.when(a == 1)
    def _():
        WM[...] = wd[...]

    def wpart(x_, z_, r0=0, rows=64):
        lanes = pl.ds(pl.multiple_of((x_ // 2) * 512, 512), 512)
        return W.at[x_ % 2, z_, pl.ds(r0, rows), lanes]

    def wblock(y_):
        lanes = pl.ds(pl.multiple_of(xh * 512 + y_ * 128, 128), 128)
        return W.at[a, z, :, lanes]

    def wm_rows(y_):
        return WM.at[pl.ds(pl.multiple_of(y_ * 64, 64), 64)]

    for k in (1, 2, 3):
        send(wm_rows(yr[k]), wblock(y), s1s.at[k], s1r.at[y], dev(x, yr[k], z, c))
    wblock(y)[...] = wm_rows(y)[...]
    for k in (1, 2, 3):
        arrived(wblock(yr[k]), s1r.at[yr[k]])
    for k in (1, 7, 2, 6, 3, 5, 4):
        send(wpart(x, z), wpart(x, z), s2s.at[k], s2r.at[z], dev(x, y, zr[k], c))

    def tok_relay():
        arrived(block(TOK, yr[3], c), tkr.at[yr[3]])
        send(block(TOK, yr[3], c), block(TOK, yr[3], c), tks.at[2], tkr.at[yr[3]], yp)
        send(block(TOK, yr[3], c), block(TOK, yr[3], c), cts.at[1], ctr.at[yr[3]], mate)
        arrived(block(DY, yr[1], c), dyr.at[yr[1]])
        send(block(DY, yr[1], c), block(DY, yr[1], c), dys.at[2], dyr.at[yr[1]], ym)
        send(block(DY, yr[1], c), block(DY, yr[1], c), cds.at[1], cdr.at[yr[1]], mate)

    def x_send(k):
        part = wpart(x, zr[k])
        send(part, part, s3s.at[0, k], s3r.at[x, zr[k]], xp)
        send(part, part, s3s.at[1, k], s3r.at[x, zr[k]], xm)

    def x_relay(k):
        arrived(wpart(xr[3], zr[k]), s3r.at[xr[3], zr[k]])
        part = wpart(xr[3], zr[k], 0, 32)
        send(part, part, s3hs.at[0, k], s3hr.at[0, zr[k]], xp)
        arrived(wpart(xr[1], zr[k]), s3r.at[xr[1], zr[k]])
        part = wpart(xr[1], zr[k], 32, 32)
        send(part, part, s3hs.at[1, k], s3hr.at[1, zr[k]], xm)

    order = (0, 1, 7, 2, 6, 3, 5, 4)
    for i, k in enumerate(order):
        if k:
            arrived(wpart(x, zr[k]), s2r.at[zr[k]])
        x_send(k)
        if i >= 2:
            x_relay(order[i - 2])
        if i == 5:
            tok_relay()
    for k in order[-2:]:
        x_relay(k)

    arrived(block(DY, yr[3], c), dyr.at[yr[3]])
    send(block(DY, yr[3], c), block(DY, yr[3], c), cds.at[2], cdr.at[yr[3]], mate)
    arrived(block(TOK, yr[1], c), tkr.at[yr[1]])
    send(block(TOK, yr[1], c), block(TOK, yr[1], c), cts.at[2], ctr.at[yr[1]], mate)
    arrived(block(TOK, yr[2], c), tkr.at[yr[2]])
    send(block(TOK, yr[2], c), block(TOK, yr[2], c), cts.at[3], ctr.at[yr[2]], mate)
    arrived(block(DY, yr[2], c), dyr.at[yr[2]])
    send(block(DY, yr[2], c), block(DY, yr[2], c), cds.at[3], cdr.at[yr[2]], mate)
    for k in order:
        arrived(wpart(xr[2], zr[k], 0, 32), s3hr.at[0, zr[k]])
        arrived(wpart(xr[2], zr[k], 32, 32), s3hr.at[1, zr[k]])
    for k in (0, 1, 3, 2):
        arrived(block(TOK, yr[k], 1 - c), ctr.at[yr[k]])
        arrived(block(DY, yr[k], 1 - c), cdr.at[yr[k]])
    for cp in own:
        cp.wait()

    nt = (((1,), (1,)), ((), ()))
    tn = (((0,), (0,)), ((), ()))
    nn = (((1,), (0,)), ((), ()))

    def dwpart(x_, g):
        lanes = pl.ds(pl.multiple_of((x_ // 2) * 512, 512), 512)
        return DWS.at[x_ % 2, pl.ds(4 * g, 4), :, lanes]

    def rxpart(x_, g):
        return RX.at[x_, pl.ds(4 * g, 4)]

    for g in (0, 1):
        cols = pl.ds(256 * g, 256)
        up = W[0, 4 * g : 4 * g + 4].reshape(256, 1024)
        down = W[1, 4 * g : 4 * g + 4].reshape(256, 1024)
        for b in range(4):
            rows = pl.ds(256 * b, 256)
            pre = lax.dot_general(TOK[rows, :], up, nt, preferred_element_type=F32)
            hg = lax.dot_general(DY[rows, :], down, nt, preferred_element_type=F32)
            hid, pg = gelu_pair(pre, hg)
            HID[rows, cols] = hid
            PG[rows, cols] = pg
        dwu = lax.dot_general(PG[:, cols], TOK[...], tn, preferred_element_type=F32)
        DWS[0, 4 * g : 4 * g + 4] = dwu.astype(BF16).reshape(4, 64, 1024)
        dwd = lax.dot_general(HID[:, cols], DY[...], tn, preferred_element_type=F32)
        DWS[1, 4 * g : 4 * g + 4] = dwd.astype(BF16).reshape(4, 64, 1024)
        for k in (2, 1, 3):
            send(dwpart(xr[k], g), rxpart(x, g), rxs.at[k, g], rxr.at[x, g], dev(xr[k], y, z, c))

    up = W[0].reshape(512, 1024)

    def crows(c_):
        return pl.ds(pl.multiple_of(c_ * 512, 512), 512)

    DXS[0] = lax.dot_general(PG[crows(1 - c), :], up, nn, preferred_element_type=F32).astype(BF16)
    send(DXS.at[0], DXC, dcs, dcr, mate)
    mine = lax.dot_general(PG[crows(c), :], up, nn, preferred_element_type=F32)
    arrived(DXC, dcr)
    DXS[1] = (mine + DXC[...].astype(F32)).astype(BF16)

    def dxrows(y_):
        return DXS.at[1, pl.ds(pl.multiple_of(y_ * 128, 128), 128)]

    for k in (2, 1, 3):
        send(dxrows(yr[k]), DXY.at[y], dvs.at[k], dvr.at[y], dev(x, yr[k], z, c))

    for g in (0, 1):
        total = dwpart(x, g)[...].astype(F32)
        for k in (1, 3, 2):
            arrived(rxpart(xr[k], g), rxr.at[xr[k], g])
            total = total + rxpart(xr[k], g)[...].astype(F32)
        SX[4 * g : 4 * g + 4] = total.astype(BF16)
    for k in (4, 3, 5, 2, 6, 1, 7):
        send(SX.at[zr[k]], RZ.at[z], rzs.at[k], rzr.at[z], dev(x, y, zr[k], c))

    total = dxrows(y)[...].astype(F32)
    for k in (1, 3, 2):
        arrived(DXY.at[yr[k]], dvr.at[yr[k]])
        total = total + DXY[yr[k]].astype(F32)
    dx_o[...] = total.astype(BF16)

    total = SX[z].astype(F32)
    for k in (1, 7, 2, 6, 3, 5, 4):
        arrived(RZ.at[zr[k]], rzr.at[zr[k]])
        total = total + RZ[zr[k]].astype(F32)
    total = total.astype(BF16)
    for i in range(NY):
        FS[i] = total[:, 128 * i : 128 * (i + 1)]

    def fin(a_, y_):
        return FIN.at[a_, pl.ds(pl.multiple_of(y_ * 64, 64), 64)]

    for k in (2, 1, 3):
        send(FS.at[yr[k]], fin(a, y), fs.at[0, k], fr.at[a, y], dev(x, yr[k], z, c))
    for k in (2, 1, 3, 0):
        send(FS.at[yr[k]], fin(a, y), fs.at[1, k], fr.at[a, y], dev(xo, yr[k], z, c))
    fin(a, y)[...] = FS[y]
    for k in (1, 3, 2):
        arrived(fin(a, yr[k]), fr.at[a, yr[k]])
    for k in (0, 1, 3, 2):
        arrived(fin(1 - a, yr[k]), fr.at[1 - a, yr[k]])
    gu_o[...] = FIN[0].T
    gd_o[...] = FIN[1]
    for cp in pending:
        cp.wait_send()


def shards(tokens, out_grad, w_up, w_down):
    vmem = pl.BlockSpec(memory_space=pltpu.VMEM)
    dma = pltpu.SemaphoreType.DMA
    return pl.pallas_call(
        kernel,
        out_shape=(
            jax.ShapeDtypeStruct((128, 1024), BF16),
            jax.ShapeDtypeStruct((128, 256), BF16),
            jax.ShapeDtypeStruct((256, 128), BF16),
        ),
        in_specs=[vmem] * 4,
        out_specs=(vmem,) * 3,
        scratch_shapes=[
            pltpu.VMEM((1024, 1024), BF16),
            pltpu.VMEM((1024, 1024), BF16),
            pltpu.VMEM((2, NZ, 64, 1024), BF16),
            pltpu.VMEM((256, 128), BF16),
            pltpu.VMEM((1024, 512), BF16),
            pltpu.VMEM((1024, 512), BF16),
            pltpu.VMEM((2, NZ, 64, 1024), BF16),
            pltpu.VMEM((NX, NZ, 64, 512), BF16),
            pltpu.VMEM((NZ, 64, 512), BF16),
            pltpu.VMEM((NZ, 64, 512), BF16),
            pltpu.VMEM((NY, 64, 128), BF16),
            pltpu.VMEM((2, 256, 128), BF16),
            pltpu.VMEM((2, 512, 1024), BF16),
            pltpu.VMEM((512, 1024), BF16),
            pltpu.VMEM((NY, 128, 1024), BF16),
            dma((2,)),
            dma((3,)), dma((NY,)), dma((3,)), dma((NY,)),
            dma((4,)), dma((NY,)), dma((4,)), dma((NY,)),
            dma((NY,)), dma((NY,)), dma((NZ,)), dma((NZ,)),
            dma((2, NZ)), dma((NX, NZ)), dma((2, NZ)), dma((2, NZ)),
            dma((NX, 2)), dma((NX, 2)), dma((NZ,)), dma((NZ,)),
            dma((2, NY)), dma((2, NY)),
            dma, dma, dma((NY,)), dma((NY,)),
        ],
        compiler_params=pltpu.CompilerParams(
            collective_id=0, has_side_effects=True, vmem_limit_bytes=56 << 20
        ),
        cost_estimate=pl.CostEstimate(
            flops=5 * 2 * 1024 * 512 * 1024, bytes_accessed=2 << 20, transcendentals=1024 * 512
        ),
        name="mlp_backward",
    )(tokens, out_grad, w_up, w_down)


def solution(mesh):
    return jax.shard_map(
        shards,
        mesh=mesh,
        in_specs=(
            P(("dp", "row", "col"), None),
            P(("dp", "row", "col"), None),
            P("row", "col"),
            P("col", "row"),
        ),
        out_specs=(P(("dp", "row", "col"), None), P("row", "col"), P("col", "row")),
        check_vma=False,
    )
```

time: 267 us -> 99 us (0.37)
  waiting for transfers between devices: 150 us -> 0 us
  Pallas kernels: 0 us -> 94.3 us
  blocking collectives: 79.5 us -> 0 us
  matrix products: 17.6 us -> 0 us
  between operations: 13.8 us -> 0.65 us
  other arithmetic: 3.27 us -> 0 us
    reduce_scatter x2 -> x0, waiting for transfers between devices: 131 us -> none  [the longest x1 73.2 us: shards(): totals = lax.psum_scatter(whole, 'row', scatter_dimension=0, tiled=True)]
    pallas_call x0 -> x1, Pallas kernels: none -> 94.3 us  [shards(): pl.pallas_call(kernel, out_shape=(jax.ShapeDtypeStruct((128, 1024), BF16)...]
    all_gather x2 -> x0, blocking collectives: 66.2 us -> none  [the longest x1 35.3 us: shards(): lax.all_gather(w_up, 'row', axis=0, tiled=True)]
    all_gather x2 -> x0, waiting for transfers between devices: 17.7 us -> none  [the longest x1 17.7 us: shards(): lax.all_gather(tokens, 'col', axis=0, tiled=True)]
    dot_general x5 -> x0, matrix products: 17.6 us -> none  [the longest x1 5.34 us: shards(): pre = jnp.dot(rows_x, up_full, preferred_element_type=jnp.float32)]
    psum x1 -> x0, blocking collectives: 13.3 us -> none  [shards(): lax.psum(jnp.concatenate([inner_rows(rows_x, pre_grad), inner_rows(rows_d...]
  transfers between devices with their start and end apart: 4 -> 0, of which waited for: 3 -> 0; matrix products, arithmetic and copies ran while one was open for 4% -> 0% of each run, Pallas kernels for 0% -> 0%
where the time goes in v1:
time: 99 us; the launch traced here: 98.2 us
  Pallas kernels  94.3 us (95%)
  local copies, waits for them, and re-layouts  3.2 us (3%)
    pallas_call x1, Pallas kernels, shards(): pl.pallas_call(kernel, out_shape=(jax.ShapeDtypeStruct((128, 1024), BF16)...  94.3 us
    unnamed x7, local copies, waits for them, and re-layouts  3.2 us

profile of v1, /device:TPU:2, one launch (start us, length us, event | category | flops | bytes accessed | tf_op | source)
XLA Modules:
  0.0 98.2 jit_solution(17436040118556847452)
XLA Ops:
  0.6 94.3 %mlp_backward.1 = (bf16[128,1024]{1,0:T(8,128)(2,1)}, bf16[128,256]{1,0:T(8,128)(2,1)}, bf16[256,128]{1,0:T(8,128)(2,1)}) custom-call(bf16[128,1024]{1,0:T(8,128)(2,1)} %tok.1, bf16[128,1024]{1,0:T(8,128)(2,1)} %dy.1, bf16[128,256]{1,0:T(8,128)(2,1)} %wu.1, bf16[256,128]{1,0:T(8,128)(2,1)} %wd.1), custom_call_target="tpu_custom_call" | custom-call | flops 5368709120 | bytes 2097152 | tf_op jit(solution)/shard_map/mlp_backward/pallas_call | solution.py:258
  95.0 0.0 copy-start.1
  95.0 1.7 %copy.10 = bf16[128,1024]{1,0:T(8,128)(2,1)} copy(bf16[128,1024]{1,0:T(8,128)(2,1)} %get-tuple-element.6) | data formatting | bytes 524288
  96.7 0.0 copy-done.1
  96.7 0.0 copy-start
  96.7 0.6 copy.11
  97.3 0.2 copy-done
  97.5 0.6 copy.12
Async XLA Ops:
  95.0 1.7 %copy-start.1 = (bf16[128,256]{1,0:T(8,128)(2,1)S(1)}, bf16[128,256]{1,0:T(8,128)(2,1)}, u32[]{:S(2)}) copy-start(bf16[128,256]{1,0:T(8,128)(2,1)} %get-tuple-element.7) | copy-start | bytes 196612
  96.7 0.9 copy-start

commit v2 on v1

v2 whole, which is shorter than its diff:
```python
import functools

import jax
import jax.numpy as jnp
from jax import lax
from jax.experimental import pallas as pl
from jax.experimental.pallas import tpu as pltpu
from jax.sharding import PartitionSpec as P

MESH = pl.DeviceIdType.MESH
BF16 = jnp.bfloat16
F32 = jnp.float32
NX, NY, NZ = 4, 4, 8
ORDER = (4, 3, 5, 2, 6, 1, 7, 0)
POS = [ORDER.index(rel) for rel in range(NZ)]


def gelu_pair(pre, hid_grad):
    k = 0.7978845608028654
    sq = pre * pre
    t = jnp.tanh(pre * (k + (k * 0.044715) * sq))
    half = 0.5 * (1.0 + t)
    hidden = pre * half
    slope = half + (0.5 * pre) * (1.0 - t * t) * (k + (3.0 * k * 0.044715) * sq)
    return hidden.astype(BF16), (hid_grad * slope).astype(BF16)


def kernel(
    tok, dy, wu, wd, dx_o, gu_o, gd_o,
    TOK, DY, W, WM, PG, HID, DWS, RXA, RXB, RX, SR, SX, RZ, FS, FIN, DXS, DXC, DXY,
    ls, tks, tkr, dys, dyr, cts, ctr, cds, cdr, s1s, s1r, zps, zpr, zms, zmr, s3s, s3r, s3hs, s3hr,
    ras, rar, rbs, rbr, rds, rdr, rrs, rrr, rzs, rzr, fs, fr, dcs, dcr, dvs, dvr,
):
    a = lax.axis_index("dp")
    row = lax.axis_index("row")
    col = lax.axis_index("col")
    xh, y = row // NY, row % NY
    z, c = col // 2, col % 2
    x = xh * 2 + a
    xr = [x, (x + 1) % NX, (x + 2) % NX, (x + 3) % NX]
    yr = [y, (y + 1) % NY, (y + 2) % NY, (y + 3) % NY]
    zr = [(z + k) % NZ for k in range(NZ)]

    def dev(x_, y_, z_, c_):
        return (x_ % 2, (x_ // 2) * NY + y_, z_ * 2 + c_)

    def send(src, dst, ss, rs, to):
        cp = pltpu.make_async_remote_copy(
            src_ref=src, dst_ref=dst, send_sem=ss, recv_sem=rs, device_id=to, device_id_type=MESH
        )
        cp.start()
        pending.append(cp)

    def arrived(ref, rs):
        pltpu.make_async_remote_copy(
            src_ref=ref, dst_ref=ref, send_sem=rs, recv_sem=rs, device_id=mate, device_id_type=MESH
        ).wait_recv()

    pending = []
    mate = dev(x, y, z, 1 - c)
    yp, ym = dev(x, yr[1], z, c), dev(x, yr[3], z, c)
    xp, xm = dev(xr[1], y, z, c), dev(xr[3], y, z, c)
    zp, zm = dev(x, y, zr[1], c), dev(x, y, zr[7], c)
    xo = xh * 2 + 1 - a
    peers = (
        [mate]
        + [dev(x, yr[k], z, c) for k in (1, 2, 3)]
        + [dev(xr[k], y, z, c) for k in (1, 3)]
        + [dev(x, y, zr[k], c) for k in range(1, NZ)]
        + [dev(xo, yr[k], z, c) for k in (1, 2, 3)]
    )
    barrier = pltpu.get_barrier_semaphore()
    for p in peers:
        pl.semaphore_signal(barrier, inc=1, device_id=p, device_id_type=MESH)

    def block(ref, y_, c_):
        return ref.at[pl.ds(pl.multiple_of((c_ * NY + y_) * 128, 128), 128)]

    def lanes_of(x_):
        return pl.ds(pl.multiple_of((x_ // 2) * 512, 512), 512)

    def wpart(x_, rel, r0=0, rows=64):
        return W.at[x_ % 2, POS[rel], pl.ds(r0, rows), lanes_of(x_)]

    def wblock(y_):
        return W.at[a, POS[0], :, pl.ds(pl.multiple_of(xh * 512 + y_ * 128, 128), 128)]

    def wm_rows(y_):
        return WM.at[pl.ds(pl.multiple_of(y_ * 64, 64), 64)]

    own = [
        pltpu.make_async_copy(tok, block(TOK, y, c), ls.at[0]),
        pltpu.make_async_copy(dy, block(DY, y, c), ls.at[1]),
    ]
    for cp in own:
        cp.start()

    @pl.when(a == 0)
    def _():
        WM[...] = wu[...].T

    @pl.when(a == 1)
    def _():
        WM[...] = wd[...]

    wblock(y)[...] = wm_rows(y)[...]
    pl.semaphore_wait(barrier, len(peers))

    for k in (2, 1, 3):
        send(wm_rows(yr[k]), wblock(y), s1s.at[k], s1r.at[y], dev(x, yr[k], z, c))
    send(tok, block(TOK, y, c), tks.at[0], tkr.at[y], yp)
    send(dy, block(DY, y, c), dys.at[0], dyr.at[y], ym)
    send(dy, block(DY, y, c), dys.at[1], dyr.at[y], yp)
    send(tok, block(TOK, y, c), tks.at[1], tkr.at[y], ym)
    send(tok, block(TOK, y, c), cts.at[0], ctr.at[y], mate)
    send(dy, block(DY, y, c), cds.at[0], cdr.at[y], mate)

    def to_mate(k, t, d):
        if t:
            send(block(TOK, yr[k], c), block(TOK, yr[k], c), cts.at[k], ctr.at[yr[k]], mate)
        if d:
            send(block(DY, yr[k], c), block(DY, yr[k], c), cds.at[k], cdr.at[yr[k]], mate)

    def tok_relay():
        arrived(block(TOK, yr[3], c), tkr.at[yr[3]])
        send(block(TOK, yr[3], c), block(TOK, yr[3], c), tks.at[2], tkr.at[yr[3]], yp)
        arrived(block(DY, yr[1], c), dyr.at[yr[1]])
        send(block(DY, yr[1], c), block(DY, yr[1], c), dys.at[2], dyr.at[yr[1]], ym)
        to_mate(3, True, False)
        to_mate(1, False, True)

    def tok_second():
        arrived(block(DY, yr[3], c), dyr.at[yr[3]])
        to_mate(3, False, True)
        arrived(block(TOK, yr[1], c), tkr.at[yr[1]])
        to_mate(1, True, False)

    def tok_last():
        arrived(block(TOK, yr[2], c), tkr.at[yr[2]])
        to_mate(2, True, False)
        arrived(block(DY, yr[2], c), dyr.at[yr[2]])
        to_mate(2, False, True)

    def x_send(rel):
        part = wpart(x, rel)
        send(part, part, s3s.at[0, rel], s3r.at[0, rel], xp)
        send(part, part, s3s.at[1, rel], s3r.at[1, rel], xm)

    def x_relay(rel):
        arrived(wpart(xr[3], rel), s3r.at[0, rel])
        part = wpart(xr[3], rel, 0, 32)
        send(part, part, s3hs.at[0, rel], s3hr.at[0, rel], xp)
        arrived(wpart(xr[1], rel), s3r.at[1, rel])
        part = wpart(xr[1], rel, 32, 32)
        send(part, part, s3hs.at[1, rel], s3hr.at[1, rel], xm)

    def z_step(k):
        lo, hi = (8 - k) % 8, k
        if k == 4:
            arrived(wpart(x, 4, 0, 32), zpr.at[4])
            arrived(wpart(x, 4, 32, 32), zmr.at[4])
            x_send(4)
            return
        if k:
            arrived(wpart(x, lo), zpr.at[k])
        r0, rows = (0, 32) if k == 3 else (0, 64)
        send(wpart(x, lo, r0, rows), wpart(x, 7 - k, r0, rows), zps.at[k], zpr.at[k + 1], zp)
        if k:
            arrived(wpart(x, hi), zmr.at[k])
        r0, rows = (32, 32) if k == 3 else (0, 64)
        send(wpart(x, hi, r0, rows), wpart(x, k + 1, r0, rows), zms.at[k], zmr.at[k + 1], zm)
        x_send(lo)
        if k:
            x_send(hi)

    for k in (1, 3, 2):
        arrived(wblock(yr[k]), s1r.at[yr[k]])
    z_step(0)
    z_step(1)
    x_relay(0)
    tok_relay()
    z_step(2)
    x_relay(7)
    x_relay(1)
    z_step(3)
    tok_second()
    x_relay(6)
    z_step(4)
    x_relay(2)
    x_relay(5)
    x_relay(3)
    tok_last()
    x_relay(4)
    for k in (0, 1, 3, 2):
        arrived(block(TOK, yr[k], 1 - c), ctr.at[yr[k]])
        arrived(block(DY, yr[k], 1 - c), cdr.at[yr[k]])
    for rel in (0, 7, 1, 6, 2, 5, 3, 4):
        arrived(wpart(xr[2], rel, 0, 32), s3hr.at[0, rel])
        arrived(wpart(xr[2], rel, 32, 32), s3hr.at[1, rel])
    for cp in own:
        cp.wait()

    nt = (((1,), (1,)), ((), ()))
    tn = (((0,), (0,)), ((), ()))
    nn = (((1,), (0,)), ((), ()))

    def hidden_pass(g):
        cols = pl.ds(256 * g, 256)
        up = W[0, 4 * g : 4 * g + 4].reshape(256, 1024)
        down = W[1, 4 * g : 4 * g + 4].reshape(256, 1024)
        for b in range(4):
            rows = pl.ds(256 * b, 256)
            pre = lax.dot_general(TOK[rows, :], up, nt, preferred_element_type=F32)
            hg = lax.dot_general(DY[rows, :], down, nt, preferred_element_type=F32)
            hid, pg = gelu_pair(pre, hg)
            HID[rows, cols] = hid
            PG[rows, cols] = pg

    def weight_pass(g, i):
        cols = pl.ds(256 * g, 256)
        left, right = ((PG, TOK), (HID, DY))[i]
        grad = lax.dot_general(left[:, cols], right[...], tn, preferred_element_type=F32)
        DWS[i, 4 * g : 4 * g + 4] = grad.astype(BF16).reshape(4, 64, 1024)

    def piece(x_, p):
        return DWS.at[x_ % 2, p, :, lanes_of(x_)]

    def unit_send(u):
        pa, pb = 2 * u, 2 * u + 1
        send(piece(xr[2], pa), RXA.at[u], ras.at[u], rar.at[u], xp)
        send(piece(xr[2], pb), RXB.at[u], rbs.at[u], rbr.at[u], xm)
        send(piece(xr[1], pb), RX.at[0, pb], rds.at[0, u], rdr.at[0, u], xp)
        send(piece(xr[3], pa), RX.at[1, pa], rds.at[1, u], rdr.at[1, u], xm)

    def unit_relay(u):
        pa, pb = 2 * u, 2 * u + 1
        arrived(RXA.at[u], rar.at[u])
        SR[pa] = (piece(xr[1], pa)[...].astype(F32) + RXA[u].astype(F32)).astype(BF16)
        send(SR.at[pa], RX.at[0, pa], rrs.at[0, u], rrr.at[0, u], xp)
        arrived(RXB.at[u], rbr.at[u])
        SR[pb] = (piece(xr[3], pb)[...].astype(F32) + RXB[u].astype(F32)).astype(BF16)
        send(SR.at[pb], RX.at[1, pb], rrs.at[1, u], rrr.at[1, u], xm)

    def unit_sum(u):
        pa, pb = 2 * u, 2 * u + 1
        arrived(RX.at[1, pa], rdr.at[1, u])
        arrived(RX.at[0, pb], rdr.at[0, u])
        arrived(RX.at[0, pa], rrr.at[0, u])
        arrived(RX.at[1, pb], rrr.at[1, u])
        for p in (pa, pb):
            total = piece(x, p)[...].astype(F32) + RX[0, p].astype(F32) + RX[1, p].astype(F32)
            SX[p] = total.astype(BF16)
            rel = ORDER[p]
            if rel:
                send(SX.at[p], RZ.at[rel], rzs.at[rel], rzr.at[rel], dev(x, y, zr[rel], c))

    def crows(c_):
        return pl.ds(pl.multiple_of(c_ * 512, 512), 512)

    def dxrows(y_):
        return DXS.at[1, pl.ds(pl.multiple_of(y_ * 128, 128), 128)]

    hidden_pass(0)
    weight_pass(0, 0)
    weight_pass(0, 1)
    unit_send(0)
    unit_send(1)
    hidden_pass(1)
    weight_pass(1, 0)
    unit_relay(0)
    weight_pass(1, 1)
    unit_send(2)
    unit_send(3)
    unit_relay(1)
    up = W[0].reshape(512, 1024)
    DXS[0] = lax.dot_general(PG[crows(1 - c), :], up, nn, preferred_element_type=F32).astype(BF16)
    send(DXS.at[0], DXC, dcs, dcr, mate)
    mine = lax.dot_general(PG[crows(c), :], up, nn, preferred_element_type=F32)
    arrived(DXC, dcr)
    DXS[1] = (mine + DXC[...].astype(F32)).astype(BF16)
    for k in (2, 1, 3):
        send(dxrows(yr[k]), DXY.at[y], dvs.at[k], dvr.at[y], dev(x, yr[k], z, c))
    unit_sum(0)
    unit_relay(2)
    unit_sum(1)
    unit_relay(3)
    unit_sum(2)

    total = dxrows(y)[...].astype(F32)
    for k in (1, 3, 2):
        arrived(DXY.at[yr[k]], dvr.at[yr[k]])
        total = total + DXY[yr[k]].astype(F32)
    dx_o[...] = total.astype(BF16)

    unit_sum(3)
    total = SX[POS[0]].astype(F32)
    for k in (4, 3, 5, 2, 6, 1, 7):
        arrived(RZ.at[k], rzr.at[k])
        total = total + RZ[k].astype(F32)
    total = total.astype(BF16)
    for i in range(NY):
        FS[i] = total[:, 128 * i : 128 * (i + 1)]

    def fin(a_, y_):
        return FIN.at[a_, pl.ds(pl.multiple_of(y_ * 64, 64), 64)]

    for k in (2, 1, 3, 0):
        send(FS.at[yr[k]], fin(a, y), fs.at[1, k], fr.at[a, y], dev(xo, yr[k], z, c))
    for k in (2, 1, 3):
        send(FS.at[yr[k]], fin(a, y), fs.at[0, k], fr.at[a, y], dev(x, yr[k], z, c))
    fin(a, y)[...] = FS[y]
    for k in (1, 3, 2):
        arrived(fin(a, yr[k]), fr.at[a, yr[k]])
    for k in (0, 1, 3, 2):
        arrived(fin(1 - a, yr[k]), fr.at[1 - a, yr[k]])
    gu_o[...] = FIN[0].T
    gd_o[...] = FIN[1]
    for cp in pending:
        cp.wait_send()


def shards(tokens, out_grad, w_up, w_down):
    vmem = pl.BlockSpec(memory_space=pltpu.VMEM)
    dma = pltpu.SemaphoreType.DMA
    return pl.pallas_call(
        kernel,
        out_shape=(
            jax.ShapeDtypeStruct((128, 1024), BF16),
            jax.ShapeDtypeStruct((128, 256), BF16),
            jax.ShapeDtypeStruct((256, 128), BF16),
        ),
        in_specs=[vmem] * 4,
        out_specs=(vmem,) * 3,
        scratch_shapes=[
            pltpu.VMEM((1024, 1024), BF16),
            pltpu.VMEM((1024, 1024), BF16),
            pltpu.VMEM((2, NZ, 64, 1024), BF16),
            pltpu.VMEM((256, 128), BF16),
            pltpu.VMEM((1024, 512), BF16),
            pltpu.VMEM((1024, 512), BF16),
            pltpu.VMEM((2, NZ, 64, 1024), BF16),
            pltpu.VMEM((4, 64, 512), BF16),
            pltpu.VMEM((4, 64, 512), BF16),
            pltpu.VMEM((2, NZ, 64, 512), BF16),
            pltpu.VMEM((NZ, 64, 512), BF16),
            pltpu.VMEM((NZ, 64, 512), BF16),
            pltpu.VMEM((NZ, 64, 512), BF16),
            pltpu.VMEM((NY, 64, 128), BF16),
            pltpu.VMEM((2, 256, 128), BF16),
            pltpu.VMEM((2, 512, 1024), BF16),
            pltpu.VMEM((512, 1024), BF16),
            pltpu.VMEM((NY, 128, 1024), BF16),
            dma((2,)),
            dma((3,)), dma((NY,)), dma((3,)), dma((NY,)),
            dma((NY,)), dma((NY,)), dma((NY,)), dma((NY,)),
            dma((NY,)), dma((NY,)),
            dma((4,)), dma((5,)), dma((4,)), dma((5,)),
            dma((2, NZ)), dma((2, NZ)), dma((2, NZ)), dma((2, NZ)),
            dma((4,)), dma((4,)), dma((4,)), dma((4,)),
            dma((2, 4)), dma((2, 4)), dma((2, 4)), dma((2, 4)),
            dma((NZ,)), dma((NZ,)),
            dma((2, NY)), dma((2, NY)),
            dma, dma, dma((NY,)), dma((NY,)),
        ],
        compiler_params=pltpu.CompilerParams(
            collective_id=0, has_side_effects=True, vmem_limit_bytes=56 << 20
        ),
        cost_estimate=pl.CostEstimate(
            flops=5 * 2 * 1024 * 512 * 1024, bytes_accessed=2 << 20, transcendentals=1024 * 512
        ),
        name="mlp_backward",
    )(tokens, out_grad, w_up, w_down)


def solution(mesh):
    return jax.shard_map(
        shards,
        mesh=mesh,
        in_specs=(
            P(("dp", "row", "col"), None),
            P(("dp", "row", "col"), None),
            P("row", "col"),
            P("col", "row"),
        ),
        out_specs=(P(("dp", "row", "col"), None), P("row", "col"), P("col", "row")),
        check_vma=False,
    )
```

time: 99 us -> 76.7 us (0.77)
  Pallas kernels: 94.3 us -> 72.7 us
    pallas_call x1, Pallas kernels: 94.3 us -> 72.7 us  [shards(): pl.pallas_call(kernel, out_shape=(jax.ShapeDtypeStruct((128, 1024), BF16)...]
where the time goes in v2:
time: 76.7 us; the launch traced here: 76.6 us
  Pallas kernels  72.7 us (95%)
  local copies, waits for them, and re-layouts  3.2 us (4%)
    pallas_call x1, Pallas kernels, shards(): pl.pallas_call(kernel, out_shape=(jax.ShapeDtypeStruct((128, 1024), BF16)...  72.7 us
    unnamed x7, local copies, waits for them, and re-layouts  3.2 us

profile of v2, /device:TPU:2, one launch (start us, length us, event | category | flops | bytes accessed | tf_op | source)
XLA Modules:
  0.0 76.6 jit_solution(10142460237659886424)
XLA Ops:
  0.6 72.7 %mlp_backward.1 = (bf16[128,1024]{1,0:T(8,128)(2,1)}, bf16[128,256]{1,0:T(8,128)(2,1)}, bf16[256,128]{1,0:T(8,128)(2,1)}) custom-call(bf16[128,1024]{1,0:T(8,128)(2,1)} %tok.1, bf16[128,1024]{1,0:T(8,128)(2,1)} %dy.1, bf16[128,256]{1,0:T(8,128)(2,1)} %wu.1, bf16[256,128]{1,0:T(8,128)(2,1)} %wd.1), custom_call_target="tpu_custom_call" | custom-call | flops 5368709120 | bytes 2097152 | tf_op jit(solution)/shard_map/mlp_backward/pallas_call | solution.py:325
  73.3 0.0 copy-start.1
  73.4 1.7 %copy.10 = bf16[128,1024]{1,0:T(8,128)(2,1)} copy(bf16[128,1024]{1,0:T(8,128)(2,1)} %get-tuple-element.6) | data formatting | bytes 524288
  75.1 0.0 copy-done.1
  75.1 0.0 copy-start
  75.1 0.6 copy.11
  75.7 0.2 copy-done
  75.9 0.6 copy.12
Async XLA Ops:
  73.3 1.7 %copy-start.1 = (bf16[128,256]{1,0:T(8,128)(2,1)S(1)}, bf16[128,256]{1,0:T(8,128)(2,1)}, u32[]{:S(2)}) copy-start(bf16[128,256]{1,0:T(8,128)(2,1)} %get-tuple-element.7) | copy-start | bytes 196612
  75.1 0.9 %copy-start = (bf16[256,128]{1,0:T(8,128)(2,1)S(1)}, bf16[256,128]{1,0:T(8,128)(2,1)}, u32[]{:S(2)}) copy-start(bf16[256,128]{1,0:T(8,128)(2,1)} %get-tuple-element.8) | copy-start | bytes 196612

commit v3 on v0

v3 whole, which is shorter than its diff:
```python
import functools

import jax
import jax.numpy as jnp
from jax import lax
from jax.experimental import pallas as pl
from jax.experimental.pallas import tpu as pltpu
from jax.sharding import PartitionSpec as P

MESH = pl.DeviceIdType.MESH
BF16 = jnp.bfloat16
F32 = jnp.float32
NX, NY, NZ = 4, 4, 8
ORDER = (4, 3, 5, 2, 6, 1, 7, 0)
FULL = (0, 1, 7)
KPOS = (0, 1, 3, 2)
POS = [ORDER.index(rel) for rel in range(NZ)]


def gelu_pair(pre, hid_grad):
    k = 0.7978845608028654
    sq = pre * pre
    t = jnp.tanh(pre * (k + (k * 0.044715) * sq))
    half = 0.5 * (1.0 + t)
    hidden = pre * half
    slope = half + (0.5 * pre) * (1.0 - t * t) * (k + (3.0 * k * 0.044715) * sq)
    return hidden.astype(BF16), (hid_grad * slope).astype(BF16)


def kernel(
    tok, dy, wu, wd, dx_o, gw_o,
    TD, W, WU, WM, PH, DWS, RXA, RXB, RX, SR, SX, RZA, RZB, RZ, RF, SF, RC, SXF, RZF, FS, FIN, DXS, DXC, DXY,
    ls, tks, tkr, dys, dyr, cts, ctr, cds, cdr, s1s, s1r, zs, zrs, zfs, zfr,
    s3s, s3r, s3hs, s3hr, fcs, fcr, fms, fmr,
    ras, rar, rbs, rbr, rds, rdr, rrs, rrr, rfs, rfr, rcs, rcr, zas, zar, rzs, rzr, fs, fr, dcs, dcr, dvs, dvr,
):
    a = lax.axis_index("dp")
    row = lax.axis_index("row")
    col = lax.axis_index("col")
    xh, y = row // NY, row % NY
    z, c = col // 2, col % 2
    x = xh * 2 + a
    xr = [x, (x + 1) % NX, (x + 2) % NX, (x + 3) % NX]
    yr = [y, (y + 1) % NY, (y + 2) % NY, (y + 3) % NY]
    zr = [(z + k) % NZ for k in range(NZ)]
    TOK, DY = TD.at[0], TD.at[1]

    def dev(x_, y_, z_, c_):
        return (x_ % 2, (x_ // 2) * NY + y_, z_ * 2 + c_)

    def send(src, dst, ss, rs, to):
        cp = pltpu.make_async_remote_copy(
            src_ref=src, dst_ref=dst, send_sem=ss, recv_sem=rs, device_id=to, device_id_type=MESH
        )
        cp.start()
        pending.append(cp)

    def arrived(ref, rs):
        pltpu.make_async_remote_copy(
            src_ref=ref, dst_ref=ref, send_sem=rs, recv_sem=rs, device_id=mate, device_id_type=MESH
        ).wait_recv()

    pending = []
    mate = dev(x, y, z, 1 - c)
    yp, ym = dev(x, yr[1], z, c), dev(x, yr[3], z, c)
    xp, xm = dev(xr[1], y, z, c), dev(xr[3], y, z, c)
    zp, zm = dev(x, y, zr[1], c), dev(x, y, zr[7], c)
    xo = xh * 2 + 1 - a
    twin, across = dev(xo, y, z, c), dev(3 - x, y, z, c)
    peers = (
        [mate]
        + [dev(x, yr[k], z, c) for k in (1, 2, 3)]
        + [dev(xr[k], y, z, c) for k in (1, 3)]
        + [dev(x, y, zr[k], c) for k in range(1, NZ)]
        + [dev(xo, yr[k], z, c) for k in (1, 2, 3)]
    )
    barrier = pltpu.get_barrier_semaphore()
    for p in peers:
        pl.semaphore_signal(barrier, inc=1, device_id=p, device_id_type=MESH)

    def block(ref, k, o):
        return ref.at[pl.ds(o * 512 + KPOS[k] * 128, 128)]

    def half(h):
        return pl.ds(pl.multiple_of(h * 512, 512), 512)

    def wpart(x_, rel, r0=0, rows=64):
        return W.at[x_ % 2, POS[rel], pl.ds(r0, rows), half(x_ // 2)]

    def warr(i, h, rel):
        return W.at[i, POS[rel], :, half(h)]

    def wblock(y_):
        return W.at[:, POS[0], :, pl.ds(pl.multiple_of(xh * 512 + y_ * 128, 128), 128)]

    def wm_rows(y_):
        return WM.at[:, pl.ds(pl.multiple_of(y_ * 64, 64), 64)]

    own = [
        pltpu.make_async_copy(wu, WU, ls.at[0]),
        pltpu.make_async_copy(wd, WM.at[1], ls.at[1]),
        pltpu.make_async_copy(tok, block(TOK, 0, 0), ls.at[2]),
        pltpu.make_async_copy(dy, block(DY, 0, 0), ls.at[3]),
    ]
    for cp in own:
        cp.start()
    own[0].wait()
    WM[0] = WU[...].T
    own[1].wait()
    wblock(y)[...] = wm_rows(y)[...]
    own[2].wait()
    own[3].wait()
    pl.semaphore_wait(barrier, len(peers))

    for k in (2, 1, 3):
        send(wm_rows(yr[k]), wblock(y), s1s.at[k], s1r.at[y], dev(x, yr[k], z, c))
    tok0, dy0 = block(TOK, 0, 0), block(DY, 0, 0)
    send(tok0, block(TOK, 3, 0), tks.at[0], tkr.at[3], yp)
    send(dy0, block(DY, 1, 0), dys.at[0], dyr.at[1], ym)
    send(dy0, block(DY, 3, 0), dys.at[1], dyr.at[3], yp)
    send(tok0, block(TOK, 1, 0), tks.at[1], tkr.at[1], ym)

    def to_mate(k, t, d):
        if t:
            send(block(TOK, k, 0), block(TOK, k, 1), cts.at[k], ctr.at[k], mate)
        if d:
            send(block(DY, k, 0), block(DY, k, 1), cds.at[k], cdr.at[k], mate)

    def tok_relay():
        arrived(block(TOK, 3, 0), tkr.at[3])
        send(block(TOK, 3, 0), block(TOK, 2, 0), tks.at[2], tkr.at[2], yp)
        arrived(block(DY, 1, 0), dyr.at[1])
        send(block(DY, 1, 0), block(DY, 2, 0), dys.at[2], dyr.at[2], ym)
        to_mate(3, True, False)
        to_mate(1, False, True)

    def tok_second():
        arrived(block(DY, 3, 0), dyr.at[3])
        to_mate(3, False, True)
        arrived(block(TOK, 1, 0), tkr.at[1])
        to_mate(1, True, False)

    def tok_last():
        arrived(block(TOK, 2, 0), tkr.at[2])
        to_mate(2, True, False)
        arrived(block(DY, 2, 0), dyr.at[2])
        to_mate(2, False, True)

    def mate_done(*ks):
        for k in ks:
            arrived(block(TOK, k, 1), ctr.at[k])
            arrived(block(DY, k, 1), cdr.at[k])

    def x_send(rel):
        part = wpart(x, rel)
        if rel in FULL:
            send(part, part, fcs.at[rel], fcr.at[rel], across)
        else:
            send(part, part, s3s.at[0, rel], s3r.at[0, rel], xp)
            send(part, part, s3s.at[1, rel], s3r.at[1, rel], xm)

    def x_relay(rel):
        if rel in FULL:
            part = warr(1 - a, 1 - xh, rel)
            arrived(part, fcr.at[rel])
            send(part, part, fms.at[rel], fmr.at[rel], twin)
            return
        arrived(wpart(xr[3], rel), s3r.at[0, rel])
        part = wpart(xr[3], rel, 0, 32)
        send(part, part, s3hs.at[0, rel], s3hr.at[0, rel], xp)
        arrived(wpart(xr[1], rel), s3r.at[1, rel])
        part = wpart(xr[1], rel, 32, 32)
        send(part, part, s3hs.at[1, rel], s3hr.at[1, rel], xm)

    def x_done(rel):
        if rel in FULL:
            arrived(warr(a, 1 - xh, rel), fmr.at[rel])
        else:
            arrived(wpart(xr[2], rel, 0, 32), s3hr.at[0, rel])
            arrived(wpart(xr[2], rel, 32, 32), s3hr.at[1, rel])

    nt = (((1,), (1,)), ((), ()))
    tn = (((0,), (0,)), ((), ()))
    nn = (((1,), (0,)), ((), ()))

    def hidden_pass(g, *blocks):
        cols = pl.ds(256 * g, 256)
        up = W[0, 4 * g : 4 * g + 4].reshape(256, 1024)
        down = W[1, 4 * g : 4 * g + 4].reshape(256, 1024)
        for b in blocks:
            rows = pl.ds(256 * b, 256)
            pre = lax.dot_general(TOK[rows, :], up, nt, preferred_element_type=F32)
            hg = lax.dot_general(DY[rows, :], down, nt, preferred_element_type=F32)
            hid, pg = gelu_pair(pre, hg)
            PH[1, rows, cols] = hid
            PH[0, rows, cols] = pg

    def z_sends():
        for k in (1, 7, 2, 6):
            send(wpart(x, 0), wpart(x, 8 - k), zs.at[k], zrs.at[8 - k], dev(x, y, zr[k], c))
        other = warr(1 - a, xh, 0)
        send(other, warr(1 - a, xh, 7), zfs.at[0], zfr.at[0], zp)
        send(other, warr(1 - a, xh, 1), zfs.at[1], zfr.at[1], zm)

    def z_relay():
        arrived(wpart(x, 6), zrs.at[6])
        send(wpart(x, 6), wpart(x, 5), zs.at[5], zrs.at[5], zp)
        send(wpart(x, 6, 0, 32), wpart(x, 4, 0, 32), zs.at[4], zrs.at[4], dev(x, y, zr[2], c))
        arrived(wpart(x, 2), zrs.at[2])
        send(wpart(x, 2), wpart(x, 3), zs.at[3], zrs.at[3], zm)
        send(wpart(x, 2, 32, 32), wpart(x, 4, 32, 32), zs.at[0], zrs.at[0], dev(x, y, zr[6], c))
        x_send(6)
        x_send(2)

    def z_step(*rels):
        for rel in rels:
            arrived(wpart(x, rel), zrs.at[rel])
            x_send(rel)

    for k in (1, 3, 2):
        arrived(wblock(yr[k]), s1r.at[yr[k]])
    x_send(0)
    z_sends()
    to_mate(0, True, True)
    z_step(7, 1)
    x_relay(0)
    z_relay()
    tok_relay()
    x_relay(7)
    x_relay(1)
    z_step(5, 3)
    arrived(wpart(x, 4, 0, 32), zrs.at[4])
    arrived(wpart(x, 4, 32, 32), zrs.at[0])
    x_send(4)
    x_relay(6)
    x_relay(2)
    tok_second()
    x_relay(5)
    x_relay(3)
    arrived(warr(1 - a, xh, 7), zfr.at[0])
    arrived(warr(1 - a, xh, 1), zfr.at[1])
    for rel in (0, 7, 1, 6):
        x_done(rel)
    x_relay(4)
    mate_done(0, 1)
    hidden_pass(1, 0, 2)
    tok_last()
    for rel in (2, 5, 3, 4):
        x_done(rel)

    def weight_pass(g, i, h):
        left = PH[i, :, pl.ds(256 * g, 256)]
        grad = lax.dot_general(left, TD[i, :, half(h)], tn, preferred_element_type=F32)
        DWS[i, 4 * g : 4 * g + 4, :, half(h)] = grad.astype(BF16).reshape(4, 64, 512)

    def piece(x_, p, r0=0, rows=64):
        return DWS.at[x_ % 2, p, pl.ds(r0, rows), half(x_ // 2)]

    def add(*refs):
        total = refs[0][...].astype(F32)
        for ref in refs[1:]:
            total = total + ref[...].astype(F32)
        return total.astype(BF16)

    def far_send(p):
        send(piece(xr[2], p, 0, 32), RXA.at[p], ras.at[p], rar.at[p], xp)
        send(piece(xr[2], p, 32, 32), RXB.at[p], rbs.at[p], rbr.at[p], xm)

    def near_send(p):
        send(piece(xr[1], p, 32, 32), RX.at[0, p, pl.ds(32, 32)], rds.at[0, p], rdr.at[0, p], xp)
        send(piece(xr[3], p, 0, 32), RX.at[1, p, pl.ds(0, 32)], rds.at[1, p], rdr.at[1, p], xm)

    def x_pass(p):
        arrived(RXA.at[p], rar.at[p])
        SR[p, 0:32] = add(piece(xr[1], p, 0, 32), RXA.at[p])
        send(SR.at[p, pl.ds(0, 32)], RX.at[0, p, pl.ds(0, 32)], rrs.at[0, p], rrr.at[0, p], xp)
        arrived(RXB.at[p], rbr.at[p])
        SR[p, 32:64] = add(piece(xr[3], p, 32, 32), RXB.at[p])
        send(SR.at[p, pl.ds(32, 32)], RX.at[1, p, pl.ds(32, 32)], rrs.at[1, p], rrr.at[1, p], xm)

    def x_sum(p):
        arrived(RX.at[0, p, pl.ds(32, 32)], rdr.at[0, p])
        arrived(RX.at[1, p, pl.ds(0, 32)], rdr.at[1, p])
        arrived(RX.at[0, p, pl.ds(0, 32)], rrr.at[0, p])
        arrived(RX.at[1, p, pl.ds(32, 32)], rrr.at[1, p])
        SX[p] = add(piece(x, p), RX.at[0, p], RX.at[1, p])

    def z_far():
        send(SX.at[0, pl.ds(0, 32)], RZA.at[0], zas.at[0], zar.at[0], dev(x, y, zr[2], c))
        send(SX.at[0, pl.ds(32, 32)], RZA.at[1], zas.at[1], zar.at[1], dev(x, y, zr[6], c))
        send(SX.at[1], RZB.at[0], zas.at[2], zar.at[2], zp)
        send(SX.at[2], RZB.at[1], zas.at[3], zar.at[3], zm)

    def z_near(p):
        i = p - 3
        arrived(RZB.at[i], zar.at[2 + i])
        arrived(RZA.at[i], zar.at[i])
        own_rows, other_rows = pl.ds(32 * i, 32), pl.ds(32 - 32 * i, 32)
        SX[p, own_rows] = add(SX.at[p, own_rows], RZB.at[i, own_rows], RZA.at[i])
        SX[p, other_rows] = add(SX.at[p, other_rows], RZB.at[i, other_rows])
        rel = ORDER[p]
        send(SX.at[p], RZ.at[i], rzs.at[rel], rzr.at[rel], dev(x, y, zr[rel], c))

    def twin_send(p):
        send(DWS.at[a, p, :, half(1 - xh)], RF.at[p - 5], rfs.at[p - 5], rfr.at[p - 5], twin)

    def twin_pass(p):
        q = p - 5
        arrived(RF.at[q], rfr.at[q])
        SF[q] = add(DWS.at[1 - a, p, :, half(1 - xh)], RF.at[q])
        send(SF.at[q], RC.at[q], rcs.at[q], rcr.at[q], across)

    def full_sum(p):
        q = p - 5
        arrived(RC.at[q], rcr.at[q])
        SXF[q, a] = add(DWS.at[a, p, :, half(xh)], RC.at[q])
        SXF[q, 1 - a] = DWS[1 - a, p, :, half(xh)]
        rel = ORDER[p]
        if rel:
            send(SXF.at[q], RZF.at[q], rzs.at[rel], rzr.at[rel], dev(x, y, zr[rel], c))

    def dxrows(k):
        return DXS.at[1, pl.ds(KPOS[k] * 128, 128)]

    hidden_pass(0, 0, 2, 1)
    mate_done(3, 2)
    hidden_pass(0, 3)
    weight_pass(0, a, 1 - xh)
    for p in range(3):
        far_send(p)
    weight_pass(0, 1 - a, 1 - xh)
    weight_pass(0, 1 - a, xh)
    for p in range(3):
        near_send(p)
    weight_pass(0, a, xh)
    far_send(3)
    hidden_pass(1, 1)
    for p in range(3):
        x_pass(p)
    near_send(3)
    hidden_pass(1, 3)
    up = W[0].reshape(512, 1024)
    DXS[0] = lax.dot_general(PH[0, 512:1024], up, nn, preferred_element_type=F32).astype(BF16)
    send(DXS.at[0], DXC, dcs, dcr, mate)
    weight_pass(1, a, 1 - xh)
    far_send(4)
    weight_pass(1, 1 - a, 1 - xh)
    weight_pass(1, 1 - a, xh)
    near_send(4)
    x_pass(3)
    for p in (5, 6, 7):
        twin_send(p)
    mine = lax.dot_general(PH[0, 0:512], up, nn, preferred_element_type=F32)
    arrived(DXC, dcr)
    DXS[1] = (mine + DXC[...].astype(F32)).astype(BF16)
    for k in (2, 1, 3):
        send(dxrows(k), DXY.at[4 - k], dvs.at[k], dvr.at[4 - k], dev(x, yr[k], z, c))
    weight_pass(1, a, xh)
    x_pass(4)
    for p in (0, 1, 2):
        x_sum(p)
    z_far()
    twin_pass(5)
    twin_pass(6)
    x_sum(3)
    twin_pass(7)
    x_sum(4)
    z_near(3)
    z_near(4)
    full_sum(5)
    full_sum(6)

    for k in (1, 3, 2):
        arrived(DXY.at[k], dvr.at[k])
    dx_o[...] = add(dxrows(0), DXY.at[1], DXY.at[3], DXY.at[2])

    full_sum(7)
    for rel in (2, 6):
        arrived(RZ.at[POS[rel] - 3], rzr.at[rel])
    for rel in (1, 7):
        arrived(RZF.at[POS[rel] - 5], rzr.at[rel])
    total = [SXF[2, i].astype(F32) + RZF[0, i].astype(F32) + RZF[1, i].astype(F32) for i in (0, 1)]
    extra = RZ[0].astype(F32) + RZ[1].astype(F32)
    total[0] = (total[0] + jnp.where(a == 0, extra, 0.0)).astype(BF16)
    total[1] = (total[1] + jnp.where(a == 1, extra, 0.0)).astype(BF16)
    for j in range(NY):
        for i in (0, 1):
            FS[j, i] = total[i][:, 128 * j : 128 * (j + 1)]

    def fin(a_, y_):
        return FIN.at[a_, :, pl.ds(pl.multiple_of(y_ * 64, 64), 64)]

    for k in (2, 1, 3, 0):
        send(FS.at[yr[k]], fin(a, y), fs.at[1, k], fr.at[a, y], dev(xo, yr[k], z, c))
    for k in (2, 1, 3):
        send(FS.at[yr[k]], fin(a, y), fs.at[0, k], fr.at[a, y], dev(x, yr[k], z, c))
    fin(a, y)[...] = FS[y]
    for k in (1, 3, 2):
        arrived(fin(a, yr[k]), fr.at[a, yr[k]])
    for k in (0, 1, 3, 2):
        arrived(fin(1 - a, yr[k]), fr.at[1 - a, yr[k]])
    gw_o[...] = (FIN[0].astype(F32) + FIN[1].astype(F32)).astype(BF16)
    for cp in pending:
        cp.wait_send()


def finish(dx, gw, dx_o, gu_o, gd_o):
    dx_o[...] = dx[...]
    gu_o[...] = gw[0].T
    gd_o[...] = gw[1]


def shards(tokens, out_grad, w_up, w_down):
    vmem = pl.BlockSpec(memory_space=pltpu.VMEM)
    dma = pltpu.SemaphoreType.DMA
    dx, gw = pl.pallas_call(
        kernel,
        out_shape=(
            jax.ShapeDtypeStruct((128, 1024), BF16),
            jax.ShapeDtypeStruct((2, 256, 128), BF16),
        ),
        in_specs=[pl.BlockSpec(memory_space=pl.ANY)] * 4,
        out_specs=(vmem,) * 2,
        scratch_shapes=[
            pltpu.VMEM((2, 1024, 1024), BF16),
            pltpu.VMEM((2, NZ, 64, 1024), BF16),
            pltpu.VMEM((128, 256), BF16),
            pltpu.VMEM((2, 256, 128), BF16),
            pltpu.VMEM((2, 1024, 512), BF16),
            pltpu.VMEM((2, NZ, 64, 1024), BF16),
            pltpu.VMEM((5, 32, 512), BF16),
            pltpu.VMEM((5, 32, 512), BF16),
            pltpu.VMEM((2, 5, 64, 512), BF16),
            pltpu.VMEM((5, 64, 512), BF16),
            pltpu.VMEM((5, 64, 512), BF16),
            pltpu.VMEM((2, 32, 512), BF16),
            pltpu.VMEM((2, 64, 512), BF16),
            pltpu.VMEM((2, 64, 512), BF16),
            pltpu.VMEM((3, 64, 512), BF16),
            pltpu.VMEM((3, 64, 512), BF16),
            pltpu.VMEM((3, 64, 512), BF16),
            pltpu.VMEM((3, 2, 64, 512), BF16),
            pltpu.VMEM((2, 2, 64, 512), BF16),
            pltpu.VMEM((NY, 2, 64, 128), BF16),
            pltpu.VMEM((2, 2, 256, 128), BF16),
            pltpu.VMEM((2, 512, 1024), BF16),
            pltpu.VMEM((512, 1024), BF16),
            pltpu.VMEM((NY, 128, 1024), BF16),
            dma((4,)),
            dma((3,)), dma((NY,)), dma((3,)), dma((NY,)),
            dma((NY,)), dma((NY,)), dma((NY,)), dma((NY,)),
            dma((NY,)), dma((NY,)),
            dma((NZ,)), dma((NZ,)),
            dma((2,)), dma((2,)),
            dma((2, NZ)), dma((2, NZ)), dma((2, NZ)), dma((2, NZ)),
            dma((NZ,)), dma((NZ,)), dma((NZ,)), dma((NZ,)),
            dma((5,)), dma((5,)), dma((5,)), dma((5,)),
            dma((2, 5)), dma((2, 5)), dma((2, 5)), dma((2, 5)),
            dma((3,)), dma((3,)), dma((3,)), dma((3,)),
            dma((4,)), dma((4,)),
            dma((NZ,)), dma((NZ,)),
            dma((2, NY)), dma((2, NY)),
            dma, dma, dma((NY,)), dma((NY,)),
        ],
        compiler_params=pltpu.CompilerParams(
            collective_id=0, has_side_effects=True, vmem_limit_bytes=56 << 20
        ),
        cost_estimate=pl.CostEstimate(
            flops=5 * 2 * 1024 * 512 * 1024, bytes_accessed=2 << 20, transcendentals=1024 * 512
        ),
        name="mlp_backward",
    )(tokens, out_grad, w_up, w_down)
    return pl.pallas_call(
        finish,
        out_shape=(
            jax.ShapeDtypeStruct((128, 1024), BF16),
            jax.ShapeDtypeStruct((128, 256), BF16),
            jax.ShapeDtypeStruct((256, 128), BF16),
        ),
        in_specs=[vmem] * 2,
        out_specs=(vmem,) * 3,
        name="finish",
    )(dx, gw)


def solution(mesh):
    return jax.shard_map(
        shards,
        mesh=mesh,
        in_specs=(
            P(("dp", "row", "col"), None),
            P(("dp", "row", "col"), None),
            P("row", "col"),
            P("col", "row"),
        ),
        out_specs=(P(("dp", "row", "col"), None), P("row", "col"), P("col", "row")),
        check_vma=False,
    )
```

time: 267 us -> 72.3 us (0.27)
  the two profiles are of different devices: /device:TPU:2 before, /device:TPU:1 now
where the time goes in v3:
time: 72.3 us; the launch traced here: 72.2 us
  Pallas kernels  71.5 us (99%)
    pallas_call x1, Pallas kernels, shards(): pl.pallas_call(kernel, out_shape=(jax.ShapeDtypeStruct((128, 1024), BF16)...  69.8 us
    pallas_call x1, Pallas kernels, shards(): pl.pallas_call(finish, out_shape=(jax.ShapeDtypeStruct((128, 1024), BF16)...  1.74 us

profile of v3, /device:TPU:1, one launch (start us, length us, event | category | flops | bytes accessed | tf_op | source)
XLA Modules:
  0.0 72.2 jit_solution(15438612949097670336)
XLA Ops:
  0.6 69.8 %mlp_backward.1 = (bf16[128,1024]{1,0:T(8,128)(2,1)}, bf16[2,256,128]{2,1,0:T(8,128)(2,1)}) custom-call(bf16[128,1024]{1,0:T(8,128)(2,1)} %tok.1, bf16[128,1024]{1,0:T(8,128)(2,1)} %dy.1, bf16[128,256]{1,0:T(8,128)(2,1)} %wu.1, bf16[256,128]{1,0:T(8,128)(2,1)} %wd.1), custom_call_target="tpu_custom_call" | custom-call | flops 5368709120 | bytes 2097152 | tf_op jit(solution)/shard_map/mlp_backward/pallas_call | solution.py:416
  70.4 1.7 %finish.1 = (bf16[128,1024]{1,0:T(8,128)(2,1)}, bf16[128,256]{1,0:T(8,128)(2,1)}, bf16[256,128]{1,0:T(8,128)(2,1)}) custom-call(bf16[128,1024]{1,0:T(8,128)(2,1)} %get-tuple-element.5.dx, bf16[2,256,128]{2,1,0:T(8,128)(2,1)} %get-tuple-element.6.gw), custom_call_target="tpu_custom_call" | custom-call | tf_op jit(solution)/shard_map/finish/pallas_call | solution.py:473

commit v4 on v3

--- a/solution.py
+++ b/solution.py
@@ -29,7 +29,7 @@
 
 def kernel(
     tok, dy, wu, wd, dx_o, gw_o,
-    TD, W, WU, WM, PH, DWS, RXA, RXB, RX, SR, SX, RZA, RZB, RZ, RF, SF, RC, SXF, RZF, FS, FIN, DXS, DXC, DXY,
+    TD, W, WU, WM, PH, DWS, RXA, RXB, RX, SR, SX, RZA, RZB, RZ, RF, SF, RC, SXF, RZF, FS, FIN, ACC, DXS, DXC, DXY,
     ls, tks, tkr, dys, dyr, cts, ctr, cds, cdr, s1s, s1r, zs, zrs, zfs, zfr,
     s3s, s3r, s3hs, s3hr, fcs, fcr, fms, fmr,
     ras, rar, rbs, rbr, rds, rdr, rrs, rrr, rfs, rfr, rcs, rcr, zas, zar, rzs, rzr, fs, fr, dcs, dcr, dvs, dvr,
@@ -112,39 +112,47 @@
     own[3].wait()
     pl.semaphore_wait(barrier, len(peers))
 
-    for k in (2, 1, 3):
-        send(wm_rows(yr[k]), wblock(y), s1s.at[k], s1r.at[y], dev(x, yr[k], z, c))
+    def first_send():
+        for k in (2, 1, 3):
+            send(wm_rows(yr[k]), wblock(y), s1s.at[k], s1r.at[y], dev(x, yr[k], z, c))
+
+    def first_done():
+        for k in (1, 3, 2):
+            arrived(wblock(yr[k]), s1r.at[yr[k]])
+
     tok0, dy0 = block(TOK, 0, 0), block(DY, 0, 0)
-    send(tok0, block(TOK, 3, 0), tks.at[0], tkr.at[3], yp)
-    send(dy0, block(DY, 1, 0), dys.at[0], dyr.at[1], ym)
-    send(dy0, block(DY, 3, 0), dys.at[1], dyr.at[3], yp)
-    send(tok0, block(TOK, 1, 0), tks.at[1], tkr.at[1], ym)
-
-    def to_mate(k, t, d):
-        if t:
-            send(block(TOK, k, 0), block(TOK, k, 1), cts.at[k], ctr.at[k], mate)
-        if d:
-            send(block(DY, k, 0), block(DY, k, 1), cds.at[k], cdr.at[k], mate)
+
+    def tok_up():
+        send(tok0, block(TOK, 3, 0), tks.at[0], tkr.at[3], yp)
+
+    def tok_down():
+        send(tok0, block(TOK, 1, 0), tks.at[1], tkr.at[1], ym)
+
+    def dy_up():
+        send(dy0, block(DY, 3, 0), dys.at[1], dyr.at[3], yp)
+
+    def dy_down():
+        send(dy0, block(DY, 1, 0), dys.at[0], dyr.at[1], ym)
+
+    def tok_done(k):
+        arrived(block(TOK, k, 0), tkr.at[k])
+
+    def dy_done(k):
+        arrived(block(DY, k, 0), dyr.at[k])
 
     def tok_relay():
-        arrived(block(TOK, 3, 0), tkr.at[3])
+        tok_done(3)
         send(block(TOK, 3, 0), block(TOK, 2, 0), tks.at[2], tkr.at[2], yp)
-        arrived(block(DY, 1, 0), dyr.at[1])
+
+    def dy_relay():
+        dy_done(1)
         send(block(DY, 1, 0), block(DY, 2, 0), dys.at[2], dyr.at[2], ym)
-        to_mate(3, True, False)
-        to_mate(1, False, True)
-
-    def tok_second():
-        arrived(block(DY, 3, 0), dyr.at[3])
-        to_mate(3, False, True)
-        arrived(block(TOK, 1, 0), tkr.at[1])
-        to_mate(1, True, False)
-
-    def tok_last():
-        arrived(block(TOK, 2, 0), tkr.at[2])
-        to_mate(2, True, False)
-        arrived(block(DY, 2, 0), dyr.at[2])
-        to_mate(2, False, True)
+
+    def tok_mate(k):
+        send(block(TOK, k, 0), block(TOK, k, 1), cts.at[k], ctr.at[k], mate)
+
+    def dy_mate(k):
+        send(block(DY, k, 0), block(DY, k, 1), cds.at[k], cdr.at[k], mate)
 
     def mate_done(*ks):
         for k in ks:
@@ -160,14 +168,16 @@
             send(part, part, s3s.at[1, rel], s3r.at[1, rel], xm)
 
     def x_relay(rel):
-        if rel in FULL:
-            part = warr(1 - a, 1 - xh, rel)
-            arrived(part, fcr.at[rel])
-            send(part, part, fms.at[rel], fmr.at[rel], twin)
-            return
+        part = warr(1 - a, 1 - xh, rel)
+        arrived(part, fcr.at[rel])
+        send(part, part, fms.at[rel], fmr.at[rel], twin)
+
+    def x_up(rel):
         arrived(wpart(xr[3], rel), s3r.at[0, rel])
         part = wpart(xr[3], rel, 0, 32)
         send(part, part, s3hs.at[0, rel], s3hr.at[0, rel], xp)
+
+    def x_down(rel):
         arrived(wpart(xr[1], rel), s3r.at[1, rel])
         part = wpart(xr[1], rel, 32, 32)
         send(part, part, s3hs.at[1, rel], s3hr.at[1, rel], xm)
@@ -175,6 +185,8 @@
     def x_done(rel):
         if rel in FULL:
             arrived(warr(a, 1 - xh, rel), fmr.at[rel])
+            if rel:
+                arrived(warr(1 - a, xh, rel), zfr.at[rel // 4])
         else:
             arrived(wpart(xr[2], rel, 0, 32), s3hr.at[0, rel])
             arrived(wpart(xr[2], rel, 32, 32), s3hr.at[1, rel])
@@ -195,58 +207,31 @@
             PH[1, rows, cols] = hid
             PH[0, rows, cols] = pg
 
-    def z_sends():
-        for k in (1, 7, 2, 6):
+    def z_send(*ks):
+        for k in ks:
             send(wpart(x, 0), wpart(x, 8 - k), zs.at[k], zrs.at[8 - k], dev(x, y, zr[k], c))
+
+    def z_other():
         other = warr(1 - a, xh, 0)
-        send(other, warr(1 - a, xh, 7), zfs.at[0], zfr.at[0], zp)
-        send(other, warr(1 - a, xh, 1), zfs.at[1], zfr.at[1], zm)
-
-    def z_relay():
-        arrived(wpart(x, 6), zrs.at[6])
+        send(other, warr(1 - a, xh, 7), zfs.at[1], zfr.at[1], zp)
+        send(other, warr(1 - a, xh, 1), zfs.at[0], zfr.at[0], zm)
+
+    def z_done(rel):
+        arrived(wpart(x, rel), zrs.at[rel])
+
+    def z_done_4():
+        arrived(wpart(x, 4, 0, 32), zrs.at[4])
+        arrived(wpart(x, 4, 32, 32), zrs.at[0])
+
+    def z_up():
+        z_done(6)
         send(wpart(x, 6), wpart(x, 5), zs.at[5], zrs.at[5], zp)
         send(wpart(x, 6, 0, 32), wpart(x, 4, 0, 32), zs.at[4], zrs.at[4], dev(x, y, zr[2], c))
-        arrived(wpart(x, 2), zrs.at[2])
+
+    def z_down():
+        z_done(2)
         send(wpart(x, 2), wpart(x, 3), zs.at[3], zrs.at[3], zm)
         send(wpart(x, 2, 32, 32), wpart(x, 4, 32, 32), zs.at[0], zrs.at[0], dev(x, y, zr[6], c))
-        x_send(6)
-        x_send(2)
-
-    def z_step(*rels):
-        for rel in rels:
-            arrived(wpart(x, rel), zrs.at[rel])
-            x_send(rel)
-
-    for k in (1, 3, 2):
-        arrived(wblock(yr[k]), s1r.at[yr[k]])
-    x_send(0)
-    z_sends()
-    to_mate(0, True, True)
-    z_step(7, 1)
-    x_relay(0)
-    z_relay()
-    tok_relay()
-    x_relay(7)
-    x_relay(1)
-    z_step(5, 3)
-    arrived(wpart(x, 4, 0, 32), zrs.at[4])
-    arrived(wpart(x, 4, 32, 32), zrs.at[0])
-    x_send(4)
-    x_relay(6)
-    x_relay(2)
-    tok_second()
-    x_relay(5)
-    x_relay(3)
-    arrived(warr(1 - a, xh, 7), zfr.at[0])
-    arrived(warr(1 - a, xh, 1), zfr.at[1])
-    for rel in (0, 7, 1, 6):
-        x_done(rel)
-    x_relay(4)
-    mate_done(0, 1)
-    hidden_pass(1, 0, 2)
-    tok_last()
-    for rel in (2, 5, 3, 4):
-        x_done(rel)
 
     def weight_pass(g, i, h):
         left = PH[i, :, pl.ds(256 * g, 256)]
@@ -285,10 +270,14 @@
         arrived(RX.at[1, p, pl.ds(32, 32)], rrr.at[1, p])
         SX[p] = add(piece(x, p), RX.at[0, p], RX.at[1, p])
 
-    def z_far():
+    def z_far_4():
         send(SX.at[0, pl.ds(0, 32)], RZA.at[0], zas.at[0], zar.at[0], dev(x, y, zr[2], c))
         send(SX.at[0, pl.ds(32, 32)], RZA.at[1], zas.at[1], zar.at[1], dev(x, y, zr[6], c))
+
+    def z_far_up():
         send(SX.at[1], RZB.at[0], zas.at[2], zar.at[2], zp)
+
+    def z_far_down():
         send(SX.at[2], RZB.at[1], zas.at[3], zar.at[3], zm)
 
     def z_near(p):
@@ -322,84 +311,179 @@
     def dxrows(k):
         return DXS.at[1, pl.ds(KPOS[k] * 128, 128)]
 
-    hidden_pass(0, 0, 2, 1)
+    up_all = W.at[0]
+
+    def dx_mate():
+        up = up_all[...].reshape(512, 1024)
+        part = lax.dot_general(PH[0, 512:1024], up, nn, preferred_element_type=F32)
+        DXS[0] = part.astype(BF16)
+        send(DXS.at[0], DXC, dcs, dcr, mate)
+
+    def dx_own():
+        up = up_all[...].reshape(512, 1024)
+        ACC[...] = lax.dot_general(PH[0, 0:512], up, nn, preferred_element_type=F32)
+
+    def dx_send():
+        for k in (2, 1, 3):
+            send(dxrows(k), DXY.at[4 - k], dvs.at[k], dvr.at[4 - k], dev(x, yr[k], z, c))
+
+    def dx_pair():
+        arrived(DXC, dcr)
+        DXS[1] = (ACC[...] + DXC[...].astype(F32)).astype(BF16)
+
+    def dx_done():
+        for k in (1, 3, 2):
+            arrived(DXY.at[k], dvr.at[k])
+        dx_o[...] = add(dxrows(0), DXY.at[1], DXY.at[3], DXY.at[2])
+
+    def fin(a_, y_):
+        return FIN.at[a_, :, pl.ds(pl.multiple_of(y_ * 64, 64), 64)]
+
+    def total_send():
+        for rel in (2, 6):
+            arrived(RZ.at[POS[rel] - 3], rzr.at[rel])
+        for rel in (1, 7):
+            arrived(RZF.at[POS[rel] - 5], rzr.at[rel])
+        total = [SXF[2, i].astype(F32) + RZF[0, i].astype(F32) + RZF[1, i].astype(F32) for i in (0, 1)]
+        extra = RZ[0].astype(F32) + RZ[1].astype(F32)
+        total[0] = (total[0] + jnp.where(a == 0, extra, 0.0)).astype(BF16)
+        total[1] = (total[1] + jnp.where(a == 1, extra, 0.0)).astype(BF16)
+        for j in range(NY):
+            for i in (0, 1):
+                FS[j, i] = total[i][:, 128 * j : 128 * (j + 1)]
+        for k in (2, 1, 3, 0):
+            send(FS.at[yr[k]], fin(a, y), fs.at[1, k], fr.at[a, y], dev(xo, yr[k], z, c))
+        for k in (2, 1, 3):
+            send(FS.at[yr[k]], fin(a, y), fs.at[0, k], fr.at[a, y], dev(x, yr[k], z, c))
+        fin(a, y)[...] = FS[y]
+
+    def total_done():
+        for k in (1, 3, 2):
+            arrived(fin(a, yr[k]), fr.at[a, yr[k]])
+        for k in (0, 1, 3, 2):
+            arrived(fin(1 - a, yr[k]), fr.at[1 - a, yr[k]])
+        gw_o[...] = (FIN[0].astype(F32) + FIN[1].astype(F32)).astype(BF16)
+
+    first_send()
+    tok_up()
+    dy_up()
+    dy_down()
+    tok_down()
+    first_done()
+    z_send(7)
+    z_send(2)
+    z_send(6)
+    x_send(0)
+    x_relay(0)
+    z_done(1)
+    x_send(1)
+    z_up()
+    z_send(1)
+    x_send(6)
+    tok_mate(0)
+    dy_mate(0)
+    z_down()
+    dy_relay()
+    x_send(2)
+    tok_relay()
+    z_done(5)
+    x_send(5)
+    x_up(6)
+    dy_mate(1)
+    z_done(3)
+    x_send(3)
+    z_done_4()
+    x_send(4)
+    x_up(2)
+    z_done(7)
+    x_send(7)
+    tok_done(1)
+    tok_mate(1)
+    tok_mate(3)
+    x_up(5)
+    x_down(3)
+    dy_done(3)
+    dy_mate(3)
+    z_other()
+    x_up(3)
+    x_down(2)
+    x_done(0)
+    x_down(4)
+    x_up(4)
+    x_down(5)
+    x_relay(1)
+    mate_done(0, 1)
+    x_relay(7)
+    x_down(6)
+    x_done(3)
+    x_done(2)
+    tok_done(2)
+    tok_mate(2)
+    x_done(4)
+    dy_done(2)
+    dy_mate(2)
+    x_done(5)
+    hidden_pass(0, 2)
+    hidden_pass(0, 1)
+    hidden_pass(0, 0)
     mate_done(3, 2)
     hidden_pass(0, 3)
     weight_pass(0, a, 1 - xh)
-    for p in range(3):
-        far_send(p)
+    far_send(2)
+    far_send(1)
+    far_send(3)
+    far_send(0)
     weight_pass(0, 1 - a, 1 - xh)
+    x_done(7)
     weight_pass(0, 1 - a, xh)
-    for p in range(3):
-        near_send(p)
+    near_send(0)
+    x_done(6)
+    x_done(1)
+    hidden_pass(1, 2)
+    hidden_pass(1, 1)
+    hidden_pass(1, 3)
+    dx_mate()
+    near_send(1)
+    hidden_pass(1, 0)
+    weight_pass(1, a, 1 - xh)
+    twin_send(5)
+    x_pass(1)
+    twin_send(6)
+    x_pass(0)
+    x_pass(2)
     weight_pass(0, a, xh)
-    far_send(3)
-    hidden_pass(1, 1)
-    for p in range(3):
-        x_pass(p)
-    near_send(3)
-    hidden_pass(1, 3)
-    up = W[0].reshape(512, 1024)
-    DXS[0] = lax.dot_general(PH[0, 512:1024], up, nn, preferred_element_type=F32).astype(BF16)
-    send(DXS.at[0], DXC, dcs, dcr, mate)
-    weight_pass(1, a, 1 - xh)
+    near_send(2)
+    weight_pass(1, a, xh)
+    weight_pass(1, 1 - a, 1 - xh)
+    dx_own()
+    twin_pass(5)
+    dx_pair()
+    dx_send()
+    x_sum(1)
     far_send(4)
-    weight_pass(1, 1 - a, 1 - xh)
+    twin_pass(6)
+    x_sum(0)
+    z_far_up()
+    z_far_4()
+    x_pass(3)
     weight_pass(1, 1 - a, xh)
     near_send(4)
-    x_pass(3)
-    for p in (5, 6, 7):
-        twin_send(p)
-    mine = lax.dot_general(PH[0, 0:512], up, nn, preferred_element_type=F32)
-    arrived(DXC, dcr)
-    DXS[1] = (mine + DXC[...].astype(F32)).astype(BF16)
-    for k in (2, 1, 3):
-        send(dxrows(k), DXY.at[4 - k], dvs.at[k], dvr.at[4 - k], dev(x, yr[k], z, c))
-    weight_pass(1, a, xh)
+    x_sum(2)
+    z_far_down()
     x_pass(4)
-    for p in (0, 1, 2):
-        x_sum(p)
-    z_far()
-    twin_pass(5)
-    twin_pass(6)
+    near_send(3)
+    full_sum(6)
+    full_sum(5)
+    twin_send(7)
+    x_sum(4)
+    z_near(4)
     x_sum(3)
+    z_near(3)
     twin_pass(7)
-    x_sum(4)
-    z_near(3)
-    z_near(4)
-    full_sum(5)
-    full_sum(6)
-
-    for k in (1, 3, 2):
-        arrived(DXY.at[k], dvr.at[k])
-    dx_o[...] = add(dxrows(0), DXY.at[1], DXY.at[3], DXY.at[2])
-
     full_sum(7)
-    for rel in (2, 6):
-        arrived(RZ.at[POS[rel] - 3], rzr.at[rel])
-    for rel in (1, 7):
-        arrived(RZF.at[POS[rel] - 5], rzr.at[rel])
-    total = [SXF[2, i].astype(F32) + RZF[0, i].astype(F32) + RZF[1, i].astype(F32) for i in (0, 1)]
-    extra = RZ[0].astype(F32) + RZ[1].astype(F32)
-    total[0] = (total[0] + jnp.where(a == 0, extra, 0.0)).astype(BF16)
-    total[1] = (total[1] + jnp.where(a == 1, extra, 0.0)).astype(BF16)
-    for j in range(NY):
-        for i in (0, 1):
-            FS[j, i] = total[i][:, 128 * j : 128 * (j + 1)]
-
-    def fin(a_, y_):
-        return FIN.at[a_, :, pl.ds(pl.multiple_of(y_ * 64, 64), 64)]
-
-    for k in (2, 1, 3, 0):
-        send(FS.at[yr[k]], fin(a, y), fs.at[1, k], fr.at[a, y], dev(xo, yr[k], z, c))
-    for k in (2, 1, 3):
-        send(FS.at[yr[k]], fin(a, y), fs.at[0, k], fr.at[a, y], dev(x, yr[k], z, c))
-    fin(a, y)[...] = FS[y]
-    for k in (1, 3, 2):
-        arrived(fin(a, yr[k]), fr.at[a, yr[k]])
-    for k in (0, 1, 3, 2):
-        arrived(fin(1 - a, yr[k]), fr.at[1 - a, yr[k]])
-    gw_o[...] = (FIN[0].astype(F32) + FIN[1].astype(F32)).astype(BF16)
+    total_send()
+    dx_done()
+    total_done()
     for cp in pending:
         cp.wait_send()
 
@@ -443,6 +527,7 @@
             pltpu.VMEM((2, 2, 64, 512), BF16),
             pltpu.VMEM((NY, 2, 64, 128), BF16),
             pltpu.VMEM((2, 2, 256, 128), BF16),
+            pltpu.VMEM((512, 1024), F32),
             pltpu.VMEM((2, 512, 1024), BF16),
             pltpu.VMEM((512, 1024), BF16),
             pltpu.VMEM((NY, 128, 1024), BF16),

time: 72.3 us -> 66.8 us (0.924)
  the two profiles are of different devices: /device:TPU:1 before, /device:TPU:2 now
where the time goes in v4:
time: 66.8 us; the launch traced here: 66.7 us
  Pallas kernels  66.1 us (99%)
    pallas_call x1, Pallas kernels, shards(): pl.pallas_call(kernel, out_shape=(jax.ShapeDtypeStruct((128, 1024), BF16)...  64.3 us
    pallas_call x1, Pallas kernels, shards(): pl.pallas_call(finish, out_shape=(jax.ShapeDtypeStruct((128, 1024), BF16)...  1.74 us

profile of v4, /device:TPU:2, one launch (start us, length us, event | category | flops | bytes accessed | tf_op | source)
XLA Modules:
  0.0 66.7 jit_solution(2503498640238387149)
XLA Ops:
  0.6 64.3 %mlp_backward.1 = (bf16[128,1024]{1,0:T(8,128)(2,1)}, bf16[2,256,128]{2,1,0:T(8,128)(2,1)}) custom-call(bf16[128,1024]{1,0:T(8,128)(2,1)} %tok.1, bf16[128,1024]{1,0:T(8,128)(2,1)} %dy.1, bf16[128,256]{1,0:T(8,128)(2,1)} %wu.1, bf16[256,128]{1,0:T(8,128)(2,1)} %wd.1), custom_call_target="tpu_custom_call" | custom-call | flops 5368709120 | bytes 2097152 | tf_op jit(solution)/shard_map/mlp_backward/pallas_call | solution.py:500
  65.0 1.7 %finish.1 = (bf16[128,1024]{1,0:T(8,128)(2,1)}, bf16[128,256]{1,0:T(8,128)(2,1)}, bf16[256,128]{1,0:T(8,128)(2,1)}) custom-call(bf16[128,1024]{1,0:T(8,128)(2,1)} %get-tuple-element.5.dx, bf16[2,256,128]{2,1,0:T(8,128)(2,1)} %get-tuple-element.6.gw), custom_call_target="tpu_custom_call" | custom-call | tf_op jit(solution)/shard_map/finish/pallas_call | solution.py:558

commit v5 on v4

--- a/solution.py
+++ b/solution.py
@@ -12,7 +12,6 @@
 F32 = jnp.float32
 NX, NY, NZ = 4, 4, 8
 ORDER = (4, 3, 5, 2, 6, 1, 7, 0)
-FULL = (0, 1, 7)
 KPOS = (0, 1, 3, 2)
 POS = [ORDER.index(rel) for rel in range(NZ)]
 
@@ -29,10 +28,10 @@
 
 def kernel(
     tok, dy, wu, wd, dx_o, gw_o,
-    TD, W, WU, WM, PH, DWS, RXA, RXB, RX, SR, SX, RZA, RZB, RZ, RF, SF, RC, SXF, RZF, FS, FIN, ACC, DXS, DXC, DXY,
-    ls, tks, tkr, dys, dyr, cts, ctr, cds, cdr, s1s, s1r, zs, zrs, zfs, zfr,
-    s3s, s3r, s3hs, s3hr, fcs, fcr, fms, fmr,
-    ras, rar, rbs, rbr, rds, rdr, rrs, rrr, rfs, rfr, rcs, rcr, zas, zar, rzs, rzr, fs, fr, dcs, dcr, dvs, dvr,
+    TD, W, WU, WM, PH, PT, DWS, RXA, RXB, RX, SR, SX, RZA, RZB, RZ, RF, SF, RC, SXF, RZF, RZO, FS, FIN, ACC, DXS, DXC, DXY,
+    ls, tks, tkr, dys, dyr, cts, ctr, cds, cdr, s1s, s1r, zs, zrs,
+    s3s, s3r, s3hs, s3hr,
+    ras, rar, rbs, rbr, rds, rdr, rrs, rrr, rfs, rfr, rcs, rcr, zas, zar, rzs, rzr, ros, ror, fs, fr, dcs, dcr, dvs, dvr,
 ):
     a = lax.axis_index("dp")
     row = lax.axis_index("row")
@@ -87,26 +86,27 @@
     def wpart(x_, rel, r0=0, rows=64):
         return W.at[x_ % 2, POS[rel], pl.ds(r0, rows), half(x_ // 2)]
 
-    def warr(i, h, rel):
-        return W.at[i, POS[rel], :, half(h)]
-
     def wblock(y_):
-        return W.at[:, POS[0], :, pl.ds(pl.multiple_of(xh * 512 + y_ * 128, 128), 128)]
+        return W.at[a, POS[0], :, pl.ds(pl.multiple_of(xh * 512 + y_ * 128, 128), 128)]
 
     def wm_rows(y_):
-        return WM.at[:, pl.ds(pl.multiple_of(y_ * 64, 64), 64)]
+        return WM.at[pl.ds(pl.multiple_of(y_ * 64, 64), 64)]
 
     own = [
         pltpu.make_async_copy(wu, WU, ls.at[0]),
-        pltpu.make_async_copy(wd, WM.at[1], ls.at[1]),
+        pltpu.make_async_copy(wd, WM, ls.at[1]),
         pltpu.make_async_copy(tok, block(TOK, 0, 0), ls.at[2]),
         pltpu.make_async_copy(dy, block(DY, 0, 0), ls.at[3]),
     ]
     for cp in own:
         cp.start()
     own[0].wait()
-    WM[0] = WU[...].T
     own[1].wait()
+
+    @pl.when(a == 0)
+    def _():
+        WM[...] = WU[...].T
+
     wblock(y)[...] = wm_rows(y)[...]
     own[2].wait()
     own[3].wait()
@@ -160,36 +160,25 @@
             arrived(block(DY, k, 1), cdr.at[k])
 
     def x_send(rel):
-        part = wpart(x, rel)
-        if rel in FULL:
-            send(part, part, fcs.at[rel], fcr.at[rel], across)
-        else:
-            send(part, part, s3s.at[0, rel], s3r.at[0, rel], xp)
-            send(part, part, s3s.at[1, rel], s3r.at[1, rel], xm)
-
-    def x_relay(rel):
-        part = warr(1 - a, 1 - xh, rel)
-        arrived(part, fcr.at[rel])
-        send(part, part, fms.at[rel], fmr.at[rel], twin)
+        for i, (r0, to) in enumerate(((0, xp), (32, xm), (32, xp), (0, xm))):
+            part = wpart(x, rel, r0, 32)
+            send(part, part, s3s.at[i, rel], s3r.at[i, rel], to)
 
     def x_up(rel):
-        arrived(wpart(xr[3], rel), s3r.at[0, rel])
         part = wpart(xr[3], rel, 0, 32)
+        arrived(part, s3r.at[0, rel])
         send(part, part, s3hs.at[0, rel], s3hr.at[0, rel], xp)
 
     def x_down(rel):
-        arrived(wpart(xr[1], rel), s3r.at[1, rel])
         part = wpart(xr[1], rel, 32, 32)
+        arrived(part, s3r.at[1, rel])
         send(part, part, s3hs.at[1, rel], s3hr.at[1, rel], xm)
 
     def x_done(rel):
-        if rel in FULL:
-            arrived(warr(a, 1 - xh, rel), fmr.at[rel])
-            if rel:
-                arrived(warr(1 - a, xh, rel), zfr.at[rel // 4])
-        else:
-            arrived(wpart(xr[2], rel, 0, 32), s3hr.at[0, rel])
-            arrived(wpart(xr[2], rel, 32, 32), s3hr.at[1, rel])
+        arrived(wpart(xr[3], rel, 32, 32), s3r.at[2, rel])
+        arrived(wpart(xr[1], rel, 0, 32), s3r.at[3, rel])
+        arrived(wpart(xr[2], rel, 0, 32), s3hr.at[0, rel])
+        arrived(wpart(xr[2], rel, 32, 32), s3hr.at[1, rel])
 
     nt = (((1,), (1,)), ((), ()))
     tn = (((0,), (0,)), ((), ()))
@@ -204,17 +193,13 @@
             pre = lax.dot_general(TOK[rows, :], up, nt, preferred_element_type=F32)
             hg = lax.dot_general(DY[rows, :], down, nt, preferred_element_type=F32)
             hid, pg = gelu_pair(pre, hg)
-            PH[1, rows, cols] = hid
+            PT[1, cols, rows] = hid.T
+            PT[0, cols, rows] = pg.T
             PH[0, rows, cols] = pg
 
     def z_send(*ks):
         for k in ks:
             send(wpart(x, 0), wpart(x, 8 - k), zs.at[k], zrs.at[8 - k], dev(x, y, zr[k], c))
-
-    def z_other():
-        other = warr(1 - a, xh, 0)
-        send(other, warr(1 - a, xh, 7), zfs.at[1], zfr.at[1], zp)
-        send(other, warr(1 - a, xh, 1), zfs.at[0], zfr.at[0], zm)
 
     def z_done(rel):
         arrived(wpart(x, rel), zrs.at[rel])
@@ -234,8 +219,8 @@
         send(wpart(x, 2, 32, 32), wpart(x, 4, 32, 32), zs.at[0], zrs.at[0], dev(x, y, zr[6], c))
 
     def weight_pass(g, i, h):
-        left = PH[i, :, pl.ds(256 * g, 256)]
-        grad = lax.dot_general(left, TD[i, :, half(h)], tn, preferred_element_type=F32)
+        left = PT[i, pl.ds(256 * g, 256)]
+        grad = lax.dot_general(left, TD[i, :, half(h)], nn, preferred_element_type=F32)
         DWS[i, 4 * g : 4 * g + 4, :, half(h)] = grad.astype(BF16).reshape(4, 64, 512)
 
     def piece(x_, p, r0=0, rows=64):
@@ -302,188 +287,213 @@
     def full_sum(p):
         q = p - 5
         arrived(RC.at[q], rcr.at[q])
-        SXF[q, a] = add(DWS.at[a, p, :, half(xh)], RC.at[q])
-        SXF[q, 1 - a] = DWS[1 - a, p, :, half(xh)]
+        SXF[q] = add(DWS.at[a, p, :, half(xh)], RC.at[q])
         rel = ORDER[p]
         if rel:
             send(SXF.at[q], RZF.at[q], rzs.at[rel], rzr.at[rel], dev(x, y, zr[rel], c))
 
+    def own_send():
+        for i, to in ((0, zp), (1, zm)):
+            send(DWS.at[1 - a, 5 + i, :, half(xh)], RZO.at[i], ros.at[i], ror.at[i], to)
+
     def dxrows(k):
         return DXS.at[1, pl.ds(KPOS[k] * 128, 128)]
 
     up_all = W.at[0]
 
-    def dx_mate():
+    def dx_rows(i):
+        return pl.ds(256 * i, 256)
+
+    def dx_part(rows):
         up = up_all[...].reshape(512, 1024)
-        part = lax.dot_general(PH[0, 512:1024], up, nn, preferred_element_type=F32)
-        DXS[0] = part.astype(BF16)
-        send(DXS.at[0], DXC, dcs, dcr, mate)
-
-    def dx_own():
-        up = up_all[...].reshape(512, 1024)
-        ACC[...] = lax.dot_general(PH[0, 0:512], up, nn, preferred_element_type=F32)
-
-    def dx_send():
-        for k in (2, 1, 3):
+        return lax.dot_general(PH[0, rows], up, nn, preferred_element_type=F32)
+
+    def dx_mate(i):
+        DXS[0, dx_rows(i)] = dx_part(pl.ds(512 + 256 * i, 256)).astype(BF16)
+        send(DXS.at[0, dx_rows(i)], DXC.at[dx_rows(i)], dcs.at[i], dcr.at[i], mate)
+
+    def dx_own(i):
+        ACC[dx_rows(i)] = dx_part(dx_rows(i))
+
+    def dx_pair(i):
+        arrived(DXC.at[dx_rows(i)], dcr.at[i])
+        DXS[1, dx_rows(i)] = (ACC[dx_rows(i)] + DXC[dx_rows(i)].astype(F32)).astype(BF16)
+
+    def dx_send(*ks):
+        for k in ks:
             send(dxrows(k), DXY.at[4 - k], dvs.at[k], dvr.at[4 - k], dev(x, yr[k], z, c))
-
-    def dx_pair():
-        arrived(DXC, dcr)
-        DXS[1] = (ACC[...] + DXC[...].astype(F32)).astype(BF16)
 
     def dx_done():
         for k in (1, 3, 2):
             arrived(DXY.at[k], dvr.at[k])
-        dx_o[...] = add(dxrows(0), DXY.at[1], DXY.at[3], DXY.at[2])
-
-    def fin(a_, y_):
-        return FIN.at[a_, :, pl.ds(pl.multiple_of(y_ * 64, 64), 64)]
+        DXS[1, 0:128] = add(dxrows(0), DXY.at[1], DXY.at[3], DXY.at[2])
+        dx_copy.start()
+
+    dx_copy = pltpu.make_async_copy(dxrows(0), dx_o, ls.at[4])
+
+    def fin(a_, i, y_):
+        return FIN.at[a_, i, pl.ds(pl.multiple_of(y_ * 64, 64), 64)]
+
+    def to_owners(i, *refs):
+        total = add(*refs)
+        for j in range(NY):
+            FS[i, j] = total[:, 128 * j : 128 * (j + 1)]
+        for k in (2, 1, 3, 0):
+            send(FS.at[i, yr[k]], fin(a, i, y), fs.at[1, i, k], fr.at[a, i, y], dev(xo, yr[k], z, c))
+        for k in (2, 1, 3):
+            send(FS.at[i, yr[k]], fin(a, i, y), fs.at[0, i, k], fr.at[a, i, y], dev(x, yr[k], z, c))
+        fin(a, i, y)[...] = FS[i, y]
+
+    def own_total():
+        for i in (0, 1):
+            arrived(RZO.at[i], ror.at[i])
+        to_owners(1, DWS.at[1 - a, 7, :, half(xh)], RZO.at[0], RZO.at[1])
 
     def total_send():
         for rel in (2, 6):
             arrived(RZ.at[POS[rel] - 3], rzr.at[rel])
         for rel in (1, 7):
             arrived(RZF.at[POS[rel] - 5], rzr.at[rel])
-        total = [SXF[2, i].astype(F32) + RZF[0, i].astype(F32) + RZF[1, i].astype(F32) for i in (0, 1)]
-        extra = RZ[0].astype(F32) + RZ[1].astype(F32)
-        total[0] = (total[0] + jnp.where(a == 0, extra, 0.0)).astype(BF16)
-        total[1] = (total[1] + jnp.where(a == 1, extra, 0.0)).astype(BF16)
-        for j in range(NY):
-            for i in (0, 1):
-                FS[j, i] = total[i][:, 128 * j : 128 * (j + 1)]
-        for k in (2, 1, 3, 0):
-            send(FS.at[yr[k]], fin(a, y), fs.at[1, k], fr.at[a, y], dev(xo, yr[k], z, c))
-        for k in (2, 1, 3):
-            send(FS.at[yr[k]], fin(a, y), fs.at[0, k], fr.at[a, y], dev(x, yr[k], z, c))
-        fin(a, y)[...] = FS[y]
+        to_owners(0, SXF.at[2], RZF.at[0], RZF.at[1], RZ.at[0], RZ.at[1])
 
     def total_done():
-        for k in (1, 3, 2):
-            arrived(fin(a, yr[k]), fr.at[a, yr[k]])
-        for k in (0, 1, 3, 2):
-            arrived(fin(1 - a, yr[k]), fr.at[1 - a, yr[k]])
-        gw_o[...] = (FIN[0].astype(F32) + FIN[1].astype(F32)).astype(BF16)
+        for i in (1, 0):
+            for k in (1, 3, 2):
+                arrived(fin(a, i, yr[k]), fr.at[a, i, yr[k]])
+            for k in (0, 1, 3, 2):
+                arrived(fin(1 - a, i, yr[k]), fr.at[1 - a, i, yr[k]])
+        gw_o[0] = add(FIN.at[0, 0], FIN.at[1, 1])
+        gw_o[1] = add(FIN.at[1, 0], FIN.at[0, 1])
 
     first_send()
+    dy_down()
     tok_up()
     dy_up()
-    dy_down()
+    first_done()
+    z_send(2)
+    z_send(7)
+    x_send(0)
+    tok_mate(0)
+    dy_mate(0)
+    z_send(6)
+    x_up(0)
+    x_down(0)
+    z_send(1)
     tok_down()
-    first_done()
-    z_send(7)
-    z_send(2)
-    z_send(6)
-    x_send(0)
-    x_relay(0)
     z_done(1)
     x_send(1)
     z_up()
-    z_send(1)
     x_send(6)
-    tok_mate(0)
-    dy_mate(0)
+    dy_relay()
+    dy_mate(1)
+    tok_relay()
     z_down()
-    dy_relay()
     x_send(2)
-    tok_relay()
+    z_done(7)
+    x_send(7)
     z_done(5)
     x_send(5)
-    x_up(6)
-    dy_mate(1)
     z_done(3)
     x_send(3)
     z_done_4()
     x_send(4)
     x_up(2)
-    z_done(7)
-    x_send(7)
+    dy_done(3)
+    dy_mate(3)
+    x_done(0)
+    x_down(5)
+    x_down(2)
+    x_up(5)
     tok_done(1)
     tok_mate(1)
+    mate_done(0, 1)
+    x_up(4)
+    x_down(4)
+    x_down(3)
     tok_mate(3)
-    x_up(5)
-    x_down(3)
-    dy_done(3)
-    dy_mate(3)
-    z_other()
+    x_down(6)
+    x_down(1)
     x_up(3)
-    x_down(2)
-    x_done(0)
-    x_down(4)
-    x_up(4)
-    x_down(5)
-    x_relay(1)
-    mate_done(0, 1)
-    x_relay(7)
-    x_down(6)
-    x_done(3)
-    x_done(2)
+    x_up(6)
+    x_up(1)
+    x_down(7)
     tok_done(2)
     tok_mate(2)
-    x_done(4)
     dy_done(2)
     dy_mate(2)
     x_done(5)
+    x_done(2)
+    x_done(4)
+    x_up(7)
+    x_done(3)
+    hidden_pass(0, 0)
+    hidden_pass(0, 1)
     hidden_pass(0, 2)
-    hidden_pass(0, 1)
-    hidden_pass(0, 0)
     mate_done(3, 2)
     hidden_pass(0, 3)
     weight_pass(0, a, 1 - xh)
+    far_send(0)
     far_send(2)
+    far_send(3)
+    x_done(7)
+    x_done(6)
     far_send(1)
-    far_send(3)
-    far_send(0)
+    x_done(1)
+    hidden_pass(1, 1)
+    hidden_pass(1, 0)
+    hidden_pass(1, 2)
+    hidden_pass(1, 3)
+    weight_pass(1, a, 1 - xh)
+    twin_send(6)
     weight_pass(0, 1 - a, 1 - xh)
-    x_done(7)
     weight_pass(0, 1 - a, xh)
     near_send(0)
-    x_done(6)
-    x_done(1)
-    hidden_pass(1, 2)
-    hidden_pass(1, 1)
-    hidden_pass(1, 3)
-    dx_mate()
+    x_pass(0)
+    dx_mate(1)
+    dx_mate(0)
+    far_send(4)
+    x_pass(2)
+    x_pass(1)
+    dx_own(1)
+    dx_own(0)
+    weight_pass(1, 1 - a, 1 - xh)
     near_send(1)
-    hidden_pass(1, 0)
-    weight_pass(1, a, 1 - xh)
+    near_send(2)
+    twin_pass(6)
+    weight_pass(1, 1 - a, xh)
+    own_send()
+    weight_pass(0, a, xh)
+    x_sum(0)
+    z_far_4()
     twin_send(5)
-    x_pass(1)
-    twin_send(6)
-    x_pass(0)
-    x_pass(2)
-    weight_pass(0, a, xh)
-    near_send(2)
+    near_send(3)
+    x_pass(3)
+    dx_pair(1)
+    dx_send(2, 3)
+    dx_pair(0)
+    dx_send(1)
+    x_sum(1)
+    z_far_up()
     weight_pass(1, a, xh)
-    weight_pass(1, 1 - a, 1 - xh)
-    dx_own()
+    near_send(4)
+    x_pass(4)
+    x_sum(2)
+    twin_send(7)
+    z_far_down()
     twin_pass(5)
-    dx_pair()
-    dx_send()
-    x_sum(1)
-    far_send(4)
-    twin_pass(6)
-    x_sum(0)
-    z_far_up()
-    z_far_4()
-    x_pass(3)
-    weight_pass(1, 1 - a, xh)
-    near_send(4)
-    x_sum(2)
-    z_far_down()
-    x_pass(4)
-    near_send(3)
     full_sum(6)
-    full_sum(5)
-    twin_send(7)
+    own_total()
+    x_sum(3)
+    z_near(3)
     x_sum(4)
     z_near(4)
-    x_sum(3)
-    z_near(3)
     twin_pass(7)
+    full_sum(5)
     full_sum(7)
     total_send()
     dx_done()
     total_done()
+    dx_copy.wait()
     for cp in pending:
         cp.wait_send()
 
@@ -504,13 +514,14 @@
             jax.ShapeDtypeStruct((2, 256, 128), BF16),
         ),
         in_specs=[pl.BlockSpec(memory_space=pl.ANY)] * 4,
-        out_specs=(vmem,) * 2,
+        out_specs=(pl.BlockSpec(memory_space=pl.ANY), vmem),
         scratch_shapes=[
             pltpu.VMEM((2, 1024, 1024), BF16),
             pltpu.VMEM((2, NZ, 64, 1024), BF16),
             pltpu.VMEM((128, 256), BF16),
-            pltpu.VMEM((2, 256, 128), BF16),
-            pltpu.VMEM((2, 1024, 512), BF16),
+            pltpu.VMEM((256, 128), BF16),
+            pltpu.VMEM((1, 1024, 512), BF16),
+            pltpu.VMEM((2, 512, 1024), BF16),
             pltpu.VMEM((2, NZ, 64, 1024), BF16),
             pltpu.VMEM((5, 32, 512), BF16),
             pltpu.VMEM((5, 32, 512), BF16),
@@ -523,29 +534,29 @@
             pltpu.VMEM((3, 64, 512), BF16),
             pltpu.VMEM((3, 64, 512), BF16),
             pltpu.VMEM((3, 64, 512), BF16),
-            pltpu.VMEM((3, 2, 64, 512), BF16),
-            pltpu.VMEM((2, 2, 64, 512), BF16),
-            pltpu.VMEM((NY, 2, 64, 128), BF16),
+            pltpu.VMEM((3, 64, 512), BF16),
+            pltpu.VMEM((2, 64, 512), BF16),
+            pltpu.VMEM((2, 64, 512), BF16),
+            pltpu.VMEM((2, NY, 64, 128), BF16),
             pltpu.VMEM((2, 2, 256, 128), BF16),
             pltpu.VMEM((512, 1024), F32),
             pltpu.VMEM((2, 512, 1024), BF16),
             pltpu.VMEM((512, 1024), BF16),
             pltpu.VMEM((NY, 128, 1024), BF16),
-            dma((4,)),
+            dma((5,)),
             dma((3,)), dma((NY,)), dma((3,)), dma((NY,)),
             dma((NY,)), dma((NY,)), dma((NY,)), dma((NY,)),
             dma((NY,)), dma((NY,)),
             dma((NZ,)), dma((NZ,)),
-            dma((2,)), dma((2,)),
-            dma((2, NZ)), dma((2, NZ)), dma((2, NZ)), dma((2, NZ)),
-            dma((NZ,)), dma((NZ,)), dma((NZ,)), dma((NZ,)),
+            dma((4, NZ)), dma((4, NZ)), dma((2, NZ)), dma((2, NZ)),
             dma((5,)), dma((5,)), dma((5,)), dma((5,)),
             dma((2, 5)), dma((2, 5)), dma((2, 5)), dma((2, 5)),
             dma((3,)), dma((3,)), dma((3,)), dma((3,)),
             dma((4,)), dma((4,)),
             dma((NZ,)), dma((NZ,)),
-            dma((2, NY)), dma((2, NY)),
-            dma, dma, dma((NY,)), dma((NY,)),
+            dma((2,)), dma((2,)),
+            dma((2, 2, NY)), dma((2, 2, NY)),
+            dma((2,)), dma((2,)), dma((NY,)), dma((NY,)),
         ],
         compiler_params=pltpu.CompilerParams(
             collective_id=0, has_side_effects=True, vmem_limit_bytes=56 << 20

time: 66.8 us -> 65.8 us (0.985)
  Pallas kernels: 66.1 us -> 64.5 us
    pallas_call x1, Pallas kernels: 64.3 us -> 62.7 us  [shards(): pl.pallas_call(kernel, out_shape=(jax.ShapeDtypeStruct((128, 1024), BF16)...]
where the time goes in v5:
time: 65.8 us; the launch traced here: 65.1 us
  Pallas kernels  64.5 us (98%)
    pallas_call x1, Pallas kernels, shards(): pl.pallas_call(kernel, out_shape=(jax.ShapeDtypeStruct((128, 1024), BF16)...  62.7 us
    pallas_call x1, Pallas kernels, shards(): pl.pallas_call(finish, out_shape=(jax.ShapeDtypeStruct((128, 1024), BF16)...  1.74 us

profile of v5, /device:TPU:2, one launch (start us, length us, event | category | flops | bytes accessed | tf_op | source)
XLA Modules:
  0.0 65.1 jit_solution(1440867098452547329)
XLA Ops:
  0.6 62.7 %mlp_backward.1 = (bf16[128,1024]{1,0:T(8,128)(2,1)}, bf16[2,256,128]{2,1,0:T(8,128)(2,1)}) custom-call(bf16[128,1024]{1,0:T(8,128)(2,1)} %tok.1, bf16[128,1024]{1,0:T(8,128)(2,1)} %dy.1, bf16[128,256]{1,0:T(8,128)(2,1)} %wu.1, bf16[256,128]{1,0:T(8,128)(2,1)} %wd.1), custom_call_target="tpu_custom_call" | custom-call | flops 5368709120 | bytes 2097152 | tf_op jit(solution)/shard_map/mlp_backward/pallas_call | solution.py:510
  63.4 1.7 %finish.1 = (bf16[128,1024]{1,0:T(8,128)(2,1)}, bf16[128,256]{1,0:T(8,128)(2,1)}, bf16[256,128]{1,0:T(8,128)(2,1)}) custom-call(bf16[128,1024]{1,0:T(8,128)(2,1)} %get-tuple-element.5.dx, bf16[2,256,128]{2,1,0:T(8,128)(2,1)} %get-tuple-element.6.gw), custom_call_target="tpu_custom_call" | custom-call | tf_op jit(solution)/shard_map/finish/pallas_call | solution.py:569

commit v6 on v5

v6 whole, which is shorter than its diff:
```python
import math

import jax
import jax.numpy as jnp
from jax import lax
from jax.experimental import pallas as pl
from jax.experimental.pallas import tpu as pltpu
from jax.sharding import PartitionSpec as P

MESH = pl.DeviceIdType.MESH
BF16 = jnp.bfloat16
F32 = jnp.float32
NX, NY, NZ = 4, 4, 8
ORDER = (4, 3, 5, 2, 6, 1, 7, 0)
KPOS = (0, 1, 3, 2)
POS = [ORDER.index(rel) for rel in range(NZ)]


def gelu_pair(pre, hid_grad):
    k = 0.7978845608028654
    sq = pre * pre
    t = jnp.tanh(pre * (k + (k * 0.044715) * sq))
    half = 0.5 * (1.0 + t)
    hidden = pre * half
    slope = half + (0.5 * pre) * (1.0 - t * t) * (k + (3.0 * k * 0.044715) * sq)
    return hidden.astype(BF16), (hid_grad * slope).astype(BF16)


def kernel(
    tok, dy, wu, wd, dx_o, gw_o,
    TD, W, WU, WM, PH, PT, DWS, RXA, RXB, RX, SR, SX, RZA, RZB, RZ, RF, SF, RC, SXF, RZF, RZO, FS, FIN, ACC, DXS, DXC, DXY,
    ls, out, s1r, tkr, dyr, mtr, zrs, s3r, xdr, rar, rbr, xsr, rfr, rcr, zar, rzr, ror, fr, dcr, dvr,
):
    a = lax.axis_index("dp")
    row = lax.axis_index("row")
    col = lax.axis_index("col")
    xh, y = row // NY, row % NY
    z, c = col // 2, col % 2
    x = xh * 2 + a
    xr = [x, (x + 1) % NX, (x + 2) % NX, (x + 3) % NX]
    yr = [y, (y + 1) % NY, (y + 2) % NY, (y + 3) % NY]
    zr = [(z + k) % NZ for k in range(NZ)]
    TOK, DY = TD.at[0], TD.at[1]

    def dev(x_, y_, z_, c_):
        return (x_ % 2, (x_ // 2) * NY + y_, z_ * 2 + c_)

    rows_sent = [0] * 5

    def send(src, dst, kind, rs, to):
        pltpu.make_async_remote_copy(
            src_ref=src, dst_ref=dst, send_sem=out.at[kind], recv_sem=rs, device_id=to, device_id_type=MESH
        ).start()
        rows_sent[kind] += math.prod(src.shape) // 1024

    def sent(kind):
        rows = rows_sent[kind]
        ref = TD.at[0, pl.ds(0, rows)] if rows <= 1024 else TD.at[:, pl.ds(0, rows // 2)]
        if rows % 16:
            ref = WM.at[pl.ds(0, 8 * rows)]
        pltpu.make_async_remote_copy(
            src_ref=ref, dst_ref=ref, send_sem=out.at[kind], recv_sem=out.at[kind], device_id=mate,
            device_id_type=MESH,
        ).wait_send()

    def arrived(ref, rs):
        pltpu.make_async_remote_copy(
            src_ref=ref, dst_ref=ref, send_sem=rs, recv_sem=rs, device_id=mate, device_id_type=MESH
        ).wait_recv()

    mate = dev(x, y, z, 1 - c)
    yp, ym = dev(x, yr[1], z, c), dev(x, yr[3], z, c)
    xp, xm = dev(xr[1], y, z, c), dev(xr[3], y, z, c)
    zp, zm = dev(x, y, zr[1], c), dev(x, y, zr[7], c)
    xo = xh * 2 + 1 - a
    twin, across = dev(xo, y, z, c), dev(3 - x, y, z, c)
    peers = (
        [mate]
        + [dev(x, yr[k], z, c) for k in (1, 2, 3)]
        + [dev(xr[k], y, z, c) for k in (1, 3)]
        + [dev(x, y, zr[k], c) for k in range(1, NZ)]
        + [dev(xo, yr[k], z, c) for k in (1, 2, 3)]
    )
    barrier = pltpu.get_barrier_semaphore()
    for p in peers:
        pl.semaphore_signal(barrier, inc=1, device_id=p, device_id_type=MESH)

    def block(ref, k, o):
        return ref.at[pl.ds(o * 512 + KPOS[k] * 128, 128)]

    def half(h):
        return pl.ds(pl.multiple_of(h * 512, 512), 512)

    def wpart(x_, rel, r0=0, rows=64):
        return W.at[x_ % 2, POS[rel], pl.ds(r0, rows), half(x_ // 2)]

    def wblock(y_):
        return W.at[a, POS[0], :, pl.ds(pl.multiple_of(xh * 512 + y_ * 128, 128), 128)]

    def wm_rows(y_):
        return WM.at[pl.ds(pl.multiple_of(y_ * 64, 64), 64)]

    own = [
        pltpu.make_async_copy(wu, WU, ls.at[0]),
        pltpu.make_async_copy(wd, WM, ls.at[1]),
        pltpu.make_async_copy(tok, block(TOK, 0, 0), ls.at[2]),
        pltpu.make_async_copy(dy, block(DY, 0, 0), ls.at[3]),
    ]
    for cp in own:
        cp.start()
    own[0].wait()
    own[1].wait()

    @pl.when(a == 0)
    def _():
        WM[...] = WU[...].T

    wblock(y)[...] = wm_rows(y)[...]
    pl.semaphore_wait(barrier, len(peers))

    def first_send():
        for k in (2, 1, 3):
            send(wm_rows(yr[k]), wblock(y), 4, s1r, dev(x, yr[k], z, c))

    def first_done():
        arrived(WM.at[pl.ds(0, 192)], s1r)

    tok0, dy0 = block(TOK, 0, 0), block(DY, 0, 0)

    def tok_up():
        send(tok0, block(TOK, 3, 0), 0, tkr.at[3], yp)

    def tok_down():
        send(tok0, block(TOK, 1, 0), 0, tkr.at[1], ym)

    def dy_up():
        send(dy0, block(DY, 3, 0), 0, dyr.at[3], yp)

    def dy_down():
        send(dy0, block(DY, 1, 0), 0, dyr.at[1], ym)

    def tok_done(k):
        arrived(block(TOK, k, 0), tkr.at[k])

    def dy_done(k):
        arrived(block(DY, k, 0), dyr.at[k])

    def tok_relay():
        tok_done(3)
        send(block(TOK, 3, 0), block(TOK, 2, 0), 0, tkr.at[2], yp)

    def dy_relay():
        dy_done(1)
        send(block(DY, 1, 0), block(DY, 2, 0), 0, dyr.at[2], ym)

    def tok_mate(k):
        send(block(TOK, k, 0), block(TOK, k, 1), 0, mtr.at[k // 2], mate)

    def dy_mate(k):
        send(block(DY, k, 0), block(DY, k, 1), 0, mtr.at[k // 2], mate)

    def mate_done(*ks):
        arrived(TD.at[:, pl.ds(0, 256)], mtr.at[ks[0] // 2])

    def x_send(rel):
        for i, (r0, to) in enumerate(((0, xp), (32, xm), (32, xp), (0, xm))):
            part = wpart(x, rel, r0, 32)
            send(part, part, 1, s3r.at[i, rel] if i < 2 else xdr.at[rel], to)

    def x_up(rel):
        part = wpart(xr[3], rel, 0, 32)
        arrived(part, s3r.at[0, rel])
        send(part, part, 1, xdr.at[rel], xp)

    def x_down(rel):
        part = wpart(xr[1], rel, 32, 32)
        arrived(part, s3r.at[1, rel])
        send(part, part, 1, xdr.at[rel], xm)

    def x_done(rel):
        arrived(W.at[0, POS[rel]], xdr.at[rel])

    nt = (((1,), (1,)), ((), ()))
    tn = (((0,), (0,)), ((), ()))
    nn = (((1,), (0,)), ((), ()))

    def hidden_pass(g, *blocks):
        cols = pl.ds(256 * g, 256)
        up = W[0, 4 * g : 4 * g + 4].reshape(256, 1024)
        down = W[1, 4 * g : 4 * g + 4].reshape(256, 1024)
        for b in blocks:
            rows = pl.ds(256 * b, 256)
            pre = lax.dot_general(TOK[rows, :], up, nt, preferred_element_type=F32)
            hg = lax.dot_general(DY[rows, :], down, nt, preferred_element_type=F32)
            hid, pg = gelu_pair(pre, hg)
            PT[1, cols, rows] = hid.T
            PT[0, cols, rows] = pg.T
            PH[0, rows, cols] = pg

    def z_send(*ks):
        for k in ks:
            send(wpart(x, 0), wpart(x, 8 - k), 1, zrs.at[8 - k], dev(x, y, zr[k], c))

    def z_done(rel):
        arrived(wpart(x, rel), zrs.at[rel])

    def z_done_4():
        arrived(wpart(x, 4), zrs.at[4])

    def z_up():
        z_done(6)
        send(wpart(x, 6), wpart(x, 5), 1, zrs.at[5], zp)
        send(wpart(x, 6, 0, 32), wpart(x, 4, 0, 32), 1, zrs.at[4], dev(x, y, zr[2], c))

    def z_down():
        z_done(2)
        send(wpart(x, 2), wpart(x, 3), 1, zrs.at[3], zm)
        send(wpart(x, 2, 32, 32), wpart(x, 4, 32, 32), 1, zrs.at[4], dev(x, y, zr[6], c))

    def weight_pass(g, i, h):
        left = PT[i, pl.ds(256 * g, 256)]
        grad = lax.dot_general(left, TD[i, :, half(h)], nn, preferred_element_type=F32)
        DWS[i, 4 * g : 4 * g + 4, :, half(h)] = grad.astype(BF16).reshape(4, 64, 512)

    def piece(x_, p, r0=0, rows=64):
        return DWS.at[x_ % 2, p, pl.ds(r0, rows), half(x_ // 2)]

    def add(*refs):
        total = refs[0][...].astype(F32)
        for ref in refs[1:]:
            total = total + ref[...].astype(F32)
        return total.astype(BF16)

    def far_send(p):
        send(piece(xr[2], p, 0, 32), RXA.at[p], 2, rar.at[p], xp)
        send(piece(xr[2], p, 32, 32), RXB.at[p], 2, rbr.at[p], xm)

    def near_send(p):
        send(piece(xr[1], p, 32, 32), RX.at[0, p, pl.ds(32, 32)], 2, xsr.at[p], xp)
        send(piece(xr[3], p, 0, 32), RX.at[1, p, pl.ds(0, 32)], 2, xsr.at[p], xm)

    def x_pass(p):
        arrived(RXA.at[p], rar.at[p])
        SR[p, 0:32] = add(piece(xr[1], p, 0, 32), RXA.at[p])
        send(SR.at[p, pl.ds(0, 32)], RX.at[0, p, pl.ds(0, 32)], 2, xsr.at[p], xp)
        arrived(RXB.at[p], rbr.at[p])
        SR[p, 32:64] = add(piece(xr[3], p, 32, 32), RXB.at[p])
        send(SR.at[p, pl.ds(32, 32)], RX.at[1, p, pl.ds(32, 32)], 2, xsr.at[p], xm)

    def x_sum(p):
        arrived(RX.at[:, p], xsr.at[p])
        SX[p] = add(piece(x, p), RX.at[0, p], RX.at[1, p])

    def z_far_4():
        send(SX.at[0, pl.ds(0, 32)], RZA.at[0], 2, zar.at[0], dev(x, y, zr[2], c))
        send(SX.at[0, pl.ds(32, 32)], RZA.at[1], 2, zar.at[1], dev(x, y, zr[6], c))

    def z_far_up():
        send(SX.at[1], RZB.at[0], 2, zar.at[0], zp)

    def z_far_down():
        send(SX.at[2], RZB.at[1], 2, zar.at[1], zm)

    def z_near(p):
        i = p - 3
        arrived(DXC.at[pl.ds(0, 48)], zar.at[i])
        own_rows, other_rows = pl.ds(32 * i, 32), pl.ds(32 - 32 * i, 32)
        SX[p, own_rows] = add(SX.at[p, own_rows], RZB.at[i, own_rows], RZA.at[i])
        SX[p, other_rows] = add(SX.at[p, other_rows], RZB.at[i, other_rows])
        rel = ORDER[p]
        send(SX.at[p], RZ.at[i], 2, rzr, dev(x, y, zr[rel], c))

    def twin_send(p):
        send(DWS.at[a, p, :, half(1 - xh)], RF.at[p - 5], 2, rfr.at[p - 5], twin)

    def twin_pass(p):
        q = p - 5
        arrived(RF.at[q], rfr.at[q])
        SF[q] = add(DWS.at[1 - a, p, :, half(1 - xh)], RF.at[q])
        send(SF.at[q], RC.at[q], 2, rcr.at[q], across)

    def full_sum(p):
        q = p - 5
        arrived(RC.at[q], rcr.at[q])
        SXF[q] = add(DWS.at[a, p, :, half(xh)], RC.at[q])
        rel = ORDER[p]
        if rel:
            send(SXF.at[q], RZF.at[q], 2, rzr, dev(x, y, zr[rel], c))

    def own_send():
        for i, to in ((0, zp), (1, zm)):
            send(DWS.at[1 - a, 5 + i, :, half(xh)], RZO.at[i], 2, ror, to)

    def dxrows(k):
        return DXS.at[1, pl.ds(KPOS[k] * 128, 128)]

    up_all = W.at[0]

    def dx_rows(i):
        return pl.ds(256 * i, 256)

    def dx_part(rows):
        up = up_all[...].reshape(512, 1024)
        return lax.dot_general(PH[0, rows], up, nn, preferred_element_type=F32)

    def dx_mate(i):
        DXS[0, dx_rows(i)] = dx_part(pl.ds(512 + 256 * i, 256)).astype(BF16)
        send(DXS.at[0, dx_rows(i)], DXC.at[dx_rows(i)], 3, dcr.at[i], mate)

    def dx_own(i):
        ACC[dx_rows(i)] = dx_part(dx_rows(i))

    def dx_pair(i):
        arrived(DXC.at[dx_rows(i)], dcr.at[i])
        DXS[1, dx_rows(i)] = (ACC[dx_rows(i)] + DXC[dx_rows(i)].astype(F32)).astype(BF16)

    def dx_send(*ks):
        for k in ks:
            send(dxrows(k), DXY.at[4 - k], 3, dvr, dev(x, yr[k], z, c))

    def dx_done():
        arrived(DXY.at[pl.ds(1, 3)], dvr)
        DXS[1, 0:128] = add(dxrows(0), DXY.at[1], DXY.at[3], DXY.at[2])
        dx_copy.start()

    dx_copy = pltpu.make_async_copy(dxrows(0), dx_o, ls.at[4])

    def fin(a_, i, y_):
        return FIN.at[a_, i, pl.ds(pl.multiple_of(y_ * 64, 64), 64)]

    def to_owners(i, *refs):
        total = add(*refs)
        for j in range(NY):
            FS[i, j] = total[:, 128 * j : 128 * (j + 1)]
        for k in (2, 1, 3, 0):
            send(FS.at[i, yr[k]], fin(a, i, y), 3, fr, dev(xo, yr[k], z, c))
        for k in (2, 1, 3):
            send(FS.at[i, yr[k]], fin(a, i, y), 3, fr, dev(x, yr[k], z, c))
        fin(a, i, y)[...] = FS[i, y]

    def own_total():
        arrived(RZO, ror)
        to_owners(1, DWS.at[1 - a, 7, :, half(xh)], RZO.at[0], RZO.at[1])

    def total_send():
        arrived(DXC.at[pl.ds(0, 128)], rzr)
        to_owners(0, SXF.at[2], RZF.at[0], RZF.at[1], RZ.at[0], RZ.at[1])

    def total_done():
        arrived(DXC.at[pl.ds(0, 112)], fr)
        gw_o[0] = add(FIN.at[0, 0], FIN.at[1, 1])
        gw_o[1] = add(FIN.at[1, 0], FIN.at[0, 1])

    first_send()
    own[2].wait()
    own[3].wait()
    tok_up()
    dy_up()
    dy_down()
    first_done()
    z_send(7)
    z_send(2)
    tok_down()
    x_send(0)
    z_send(6)
    z_done(1)
    x_send(1)
    z_up()
    x_send(6)
    dy_relay()
    tok_relay()
    z_down()
    x_send(2)
    z_send(1)
    dy_mate(1)
    z_done(5)
    x_send(5)
    z_done(3)
    x_send(3)
    z_done_4()
    x_send(4)
    x_up(5)
    x_down(5)
    x_down(2)
    x_up(3)
    dy_done(3)
    dy_mate(3)
    x_up(2)
    tok_mate(0)
    dy_mate(0)
    x_down(3)
    x_down(4)
    tok_mate(3)
    x_up(4)
    z_done(7)
    x_send(7)
    x_down(1)
    tok_done(1)
    tok_mate(1)
    dy_done(2)
    dy_mate(2)
    tok_done(2)
    tok_mate(2)
    mate_done(0, 1)
    x_up(6)
    x_down(6)
    x_up(1)
    x_up(0)
    x_done(3)
    x_done(5)
    x_done(2)
    x_down(0)
    x_done(4)
    hidden_pass(0, 1)
    hidden_pass(0, 0)
    x_down(7)
    x_up(7)
    mate_done(3, 2)
    hidden_pass(0, 3)
    hidden_pass(0, 2)
    weight_pass(0, a, 1 - xh)
    far_send(2)
    far_send(0)
    weight_pass(0, 1 - a, 1 - xh)
    far_send(1)
    x_done(6)
    x_done(0)
    x_done(1)
    weight_pass(0, 1 - a, xh)
    near_send(0)
    x_done(7)
    hidden_pass(1, 1)
    far_send(3)
    hidden_pass(1, 0)
    x_pass(2)
    near_send(1)
    hidden_pass(1, 2)
    x_pass(0)
    hidden_pass(1, 3)
    weight_pass(1, a, 1 - xh)
    weight_pass(1, 1 - a, xh)
    twin_send(5)
    own_send()
    far_send(4)
    weight_pass(1, 1 - a, 1 - xh)
    dx_mate(1)
    twin_send(6)
    x_pass(1)
    dx_mate(0)
    near_send(2)
    x_pass(3)
    dx_own(1)
    weight_pass(0, a, xh)
    x_sum(0)
    near_send(4)
    dx_own(0)
    z_far_4()
    dx_pair(0)
    dx_send(1)
    dx_pair(1)
    dx_send(2, 3)
    twin_pass(5)
    weight_pass(1, a, xh)
    near_send(3)
    twin_pass(6)
    x_pass(4)
    x_sum(1)
    z_far_up()
    x_sum(2)
    z_far_down()
    twin_send(7)
    own_total()
    full_sum(5)
    full_sum(6)
    x_sum(3)
    x_sum(4)
    z_near(3)
    z_near(4)
    twin_pass(7)
    full_sum(7)
    total_send()
    dx_done()
    total_done()
    dx_copy.wait()
    for kind in range(5):
        sent(kind)


def finish(dx, gw, dx_o, gu_o, gd_o):
    dx_o[...] = dx[...]
    gu_o[...] = gw[0].T
    gd_o[...] = gw[1]


def shards(tokens, out_grad, w_up, w_down):
    vmem = pl.BlockSpec(memory_space=pltpu.VMEM)
    dma = pltpu.SemaphoreType.DMA
    dx, gw = pl.pallas_call(
        kernel,
        out_shape=(
            jax.ShapeDtypeStruct((128, 1024), BF16),
            jax.ShapeDtypeStruct((2, 256, 128), BF16),
        ),
        in_specs=[pl.BlockSpec(memory_space=pl.ANY)] * 4,
        out_specs=(pl.BlockSpec(memory_space=pl.ANY), vmem),
        scratch_shapes=[
            pltpu.VMEM((2, 1024, 1024), BF16),
            pltpu.VMEM((2, NZ, 64, 1024), BF16),
            pltpu.VMEM((128, 256), BF16),
            pltpu.VMEM((256, 128), BF16),
            pltpu.VMEM((1, 1024, 512), BF16),
            pltpu.VMEM((2, 512, 1024), BF16),
            pltpu.VMEM((2, NZ, 64, 1024), BF16),
            pltpu.VMEM((5, 32, 512), BF16),
            pltpu.VMEM((5, 32, 512), BF16),
            pltpu.VMEM((2, 5, 64, 512), BF16),
            pltpu.VMEM((5, 64, 512), BF16),
            pltpu.VMEM((5, 64, 512), BF16),
            pltpu.VMEM((2, 32, 512), BF16),
            pltpu.VMEM((2, 64, 512), BF16),
            pltpu.VMEM((2, 64, 512), BF16),
            pltpu.VMEM((3, 64, 512), BF16),
            pltpu.VMEM((3, 64, 512), BF16),
            pltpu.VMEM((3, 64, 512), BF16),
            pltpu.VMEM((3, 64, 512), BF16),
            pltpu.VMEM((2, 64, 512), BF16),
            pltpu.VMEM((2, 64, 512), BF16),
            pltpu.VMEM((2, NY, 64, 128), BF16),
            pltpu.VMEM((2, 2, 256, 128), BF16),
            pltpu.VMEM((512, 1024), F32),
            pltpu.VMEM((2, 512, 1024), BF16),
            pltpu.VMEM((512, 1024), BF16),
            pltpu.VMEM((NY, 128, 1024), BF16),
            dma((5,)), dma((5,)), dma,
            dma((NY,)), dma((NY,)), dma((2,)),
            dma((NZ,)), dma((2, NZ)), dma((NZ,)),
            dma((5,)), dma((5,)), dma((5,)),
            dma((3,)), dma((3,)), dma((2,)), dma, dma, dma,
            dma((2,)), dma,
        ],
        compiler_params=pltpu.CompilerParams(
            collective_id=0, has_side_effects=True, vmem_limit_bytes=56 << 20
        ),
        cost_estimate=pl.CostEstimate(
            flops=5 * 2 * 1024 * 512 * 1024, bytes_accessed=2 << 20, transcendentals=1024 * 512
        ),
        name="mlp_backward",
    )(tokens, out_grad, w_up, w_down)
    return pl.pallas_call(
        finish,
        out_shape=(
            jax.ShapeDtypeStruct((128, 1024), BF16),
            jax.ShapeDtypeStruct((128, 256), BF16),
            jax.ShapeDtypeStruct((256, 128), BF16),
        ),
        in_specs=[vmem] * 2,
        out_specs=(vmem,) * 3,
        name="finish",
    )(dx, gw)


def solution(mesh):
    return jax.shard_map(
        shards,
        mesh=mesh,
        in_specs=(
            P(("dp", "row", "col"), None),
            P(("dp", "row", "col"), None),
            P("row", "col"),
            P("col", "row"),
        ),
        out_specs=(P(("dp", "row", "col"), None), P("row", "col"), P("col", "row")),
        check_vma=False,
    )
```

time: 65.8 us -> 62.8 us (0.954)
  Pallas kernels: 64.5 us -> 61.7 us
    pallas_call x1, Pallas kernels: 62.7 us -> 60 us  [shards(): pl.pallas_call(kernel, out_shape=(jax.ShapeDtypeStruct((128, 1024), BF16)...]
where the time goes in v6:
time: 62.8 us; the launch traced here: 62.3 us
  Pallas kernels  61.7 us (98%)
  between operations  0.64 us (1%)
    pallas_call x1, Pallas kernels, shards(): pl.pallas_call(kernel, out_shape=(jax.ShapeDtypeStruct((128, 1024), BF16)...  60 us
    pallas_call x1, Pallas kernels, shards(): pl.pallas_call(finish, out_shape=(jax.ShapeDtypeStruct((128, 1024), BF16)...  1.74 us

profile of v6, /device:TPU:2, one launch (start us, length us, event | category | flops | bytes accessed | tf_op | source)
XLA Modules:
  0.0 62.3 jit_solution(9219675179499076237)
XLA Ops:
  0.6 60.0 %mlp_backward.1 = (bf16[128,1024]{1,0:T(8,128)(2,1)}, bf16[2,256,128]{2,1,0:T(8,128)(2,1)}) custom-call(bf16[128,1024]{1,0:T(8,128)(2,1)} %tok.1, bf16[128,1024]{1,0:T(8,128)(2,1)} %dy.1, bf16[128,256]{1,0:T(8,128)(2,1)} %wu.1, bf16[256,128]{1,0:T(8,128)(2,1)} %wd.1), custom_call_target="tpu_custom_call" | custom-call | flops 5368709120 | bytes 2097152 | tf_op jit(solution)/shard_map/mlp_backward/pallas_call | solution.py:498
  60.6 1.7 %finish.1 = (bf16[128,1024]{1,0:T(8,128)(2,1)}, bf16[128,256]{1,0:T(8,128)(2,1)}, bf16[256,128]{1,0:T(8,128)(2,1)}) custom-call(bf16[128,1024]{1,0:T(8,128)(2,1)} %get-tuple-element.5.dx, bf16[2,256,128]{2,1,0:T(8,128)(2,1)} %get-tuple-element.6.gw), custom_call_target="tpu_custom_call" | custom-call | tf_op jit(solution)/shard_map/finish/pallas_call | solution.py:549

commit v7 on v6

--- a/solution.py
+++ b/solution.py
@@ -28,7 +28,7 @@
 
 def kernel(
     tok, dy, wu, wd, dx_o, gw_o,
-    TD, W, WU, WM, PH, PT, DWS, RXA, RXB, RX, SR, SX, RZA, RZB, RZ, RF, SF, RC, SXF, RZF, RZO, FS, FIN, ACC, DXS, DXC, DXY,
+    TD, W, WU, WM, PH, PT, DWS, RXA, RXB, RX, SR, SX, RZA, RZB, RZ, RF, SF, RC, SXF, RZF, RZO, FS, ACC, DXS, DXC, DXY,
     ls, out, s1r, tkr, dyr, mtr, zrs, s3r, xdr, rar, rbr, xsr, rfr, rcr, zar, rzr, ror, fr, dcr, dvr,
 ):
     a = lax.axis_index("dp")
@@ -326,7 +326,7 @@
     dx_copy = pltpu.make_async_copy(dxrows(0), dx_o, ls.at[4])
 
     def fin(a_, i, y_):
-        return FIN.at[a_, i, pl.ds(pl.multiple_of(y_ * 64, 64), 64)]
+        return gw_o.at[a_, i, pl.ds(pl.multiple_of(y_ * 64, 64), 64)]
 
     def to_owners(i, *refs):
         total = add(*refs)
@@ -336,7 +336,7 @@
             send(FS.at[i, yr[k]], fin(a, i, y), 3, fr, dev(xo, yr[k], z, c))
         for k in (2, 1, 3):
             send(FS.at[i, yr[k]], fin(a, i, y), 3, fr, dev(x, yr[k], z, c))
-        fin(a, i, y)[...] = FS[i, y]
+        pltpu.make_async_copy(FS.at[i, y], fin(a, i, y), ls.at[5 + i]).start()
 
     def own_total():
         arrived(RZO, ror)
@@ -348,8 +348,8 @@
 
     def total_done():
         arrived(DXC.at[pl.ds(0, 112)], fr)
-        gw_o[0] = add(FIN.at[0, 0], FIN.at[1, 1])
-        gw_o[1] = add(FIN.at[1, 0], FIN.at[0, 1])
+        for i in (0, 1):
+            pltpu.make_async_copy(FS.at[i, y], fin(a, i, y), ls.at[5 + i]).wait()
 
     first_send()
     own[2].wait()
@@ -488,8 +488,8 @@
 
 def finish(dx, gw, dx_o, gu_o, gd_o):
     dx_o[...] = dx[...]
-    gu_o[...] = gw[0].T
-    gd_o[...] = gw[1]
+    gu_o[...] = (gw[0, 0].astype(F32) + gw[1, 1].astype(F32)).astype(BF16).T
+    gd_o[...] = (gw[1, 0].astype(F32) + gw[0, 1].astype(F32)).astype(BF16)
 
 
 def shards(tokens, out_grad, w_up, w_down):
@@ -499,10 +499,10 @@
         kernel,
         out_shape=(
             jax.ShapeDtypeStruct((128, 1024), BF16),
-            jax.ShapeDtypeStruct((2, 256, 128), BF16),
+            jax.ShapeDtypeStruct((2, 2, 256, 128), BF16),
         ),
         in_specs=[pl.BlockSpec(memory_space=pl.ANY)] * 4,
-        out_specs=(pl.BlockSpec(memory_space=pl.ANY), vmem),
+        out_specs=(pl.BlockSpec(memory_space=pl.ANY),) * 2,
         scratch_shapes=[
             pltpu.VMEM((2, 1024, 1024), BF16),
             pltpu.VMEM((2, NZ, 64, 1024), BF16),
@@ -526,12 +526,11 @@
             pltpu.VMEM((2, 64, 512), BF16),
             pltpu.VMEM((2, 64, 512), BF16),
             pltpu.VMEM((2, NY, 64, 128), BF16),
-            pltpu.VMEM((2, 2, 256, 128), BF16),
             pltpu.VMEM((512, 1024), F32),
             pltpu.VMEM((2, 512, 1024), BF16),
             pltpu.VMEM((512, 1024), BF16),
             pltpu.VMEM((NY, 128, 1024), BF16),
-            dma((5,)), dma((5,)), dma,
+            dma((7,)), dma((5,)), dma,
             dma((NY,)), dma((NY,)), dma((2,)),
             dma((NZ,)), dma((2, NZ)), dma((NZ,)),
             dma((5,)), dma((5,)), dma((5,)),

time: 62.8 us -> 62.3 us (level)
  no operation moved by 1% of the time
where the time goes in v7:
time: 62.3 us; the launch traced here: 61.8 us
  Pallas kernels  61.2 us (98%)
  between operations  0.64 us (1%)
    pallas_call x1, Pallas kernels, shards(): pl.pallas_call(kernel, out_shape=(jax.ShapeDtypeStruct((128, 1024), BF16)...  59.4 us
    pallas_call x1, Pallas kernels, shards(): pl.pallas_call(finish, out_shape=(jax.ShapeDtypeStruct((128, 1024), BF16)...  1.79 us

profile of v7, /device:TPU:2, one launch (start us, length us, event | category | flops | bytes accessed | tf_op | source)
XLA Modules:
  0.0 61.8 jit_solution(5644037927747085509)
XLA Ops:
  0.6 59.4 %mlp_backward.1 = (bf16[128,1024]{1,0:T(8,128)(2,1)}, bf16[2,2,256,128]{3,2,1,0:T(8,128)(2,1)}) custom-call(bf16[128,1024]{1,0:T(8,128)(2,1)} %tok.1, bf16[128,1024]{1,0:T(8,128)(2,1)} %dy.1, bf16[128,256]{1,0:T(8,128)(2,1)} %wu.1, bf16[256,128]{1,0:T(8,128)(2,1)} %wd.1), custom_call_target="tpu_custom_call" | custom-call | flops 5368709120 | bytes 2097152 | tf_op jit(solution)/shard_map/mlp_backward/pallas_call | solution.py:498
  60.1 1.8 %finish.1 = (bf16[128,1024]{1,0:T(8,128)(2,1)}, bf16[128,256]{1,0:T(8,128)(2,1)}, bf16[256,128]{1,0:T(8,128)(2,1)}) custom-call(bf16[128,1024]{1,0:T(8,128)(2,1)} %get-tuple-element.5.dx, bf16[2,2,256,128]{3,2,1,0:T(8,128)(2,1)} %get-tuple-element.6.gw), custom_call_target="tpu_custom_call" | custom-call | tf_op jit(solution)/shard_map/finish/pallas_call | solution.py:548

commit v8 on v7

--- a/solution.py
+++ b/solution.py
@@ -355,128 +355,128 @@
     own[2].wait()
     own[3].wait()
     tok_up()
-    dy_up()
     dy_down()
+    tok_down()
     first_done()
     z_send(7)
     z_send(2)
-    tok_down()
+    z_send(6)
     x_send(0)
-    z_send(6)
+    x_down(0)
+    x_up(0)
+    dy_up()
     z_done(1)
     x_send(1)
     z_up()
     x_send(6)
     dy_relay()
-    tok_relay()
+    z_send(1)
     z_down()
     x_send(2)
-    z_send(1)
-    dy_mate(1)
+    tok_relay()
     z_done(5)
     x_send(5)
+    tok_mate(0)
+    dy_mate(0)
     z_done(3)
     x_send(3)
     z_done_4()
     x_send(4)
+    x_up(2)
+    x_down(5)
+    x_down(3)
+    x_down(2)
     x_up(5)
-    x_down(5)
-    x_down(2)
     x_up(3)
+    dy_mate(1)
+    x_down(4)
     dy_done(3)
     dy_mate(3)
-    x_up(2)
-    tok_mate(0)
-    dy_mate(0)
-    x_down(3)
-    x_down(4)
-    tok_mate(3)
     x_up(4)
+    tok_done(1)
+    tok_mate(1)
     z_done(7)
     x_send(7)
-    x_down(1)
-    tok_done(1)
-    tok_mate(1)
+    x_down(6)
+    tok_mate(3)
+    x_done(5)
+    x_up(6)
     dy_done(2)
     dy_mate(2)
+    x_done(3)
+    mate_done(0, 1)
     tok_done(2)
     tok_mate(2)
-    mate_done(0, 1)
-    x_up(6)
-    x_down(6)
+    x_down(1)
     x_up(1)
-    x_up(0)
-    x_done(3)
-    x_done(5)
     x_done(2)
-    x_down(0)
     x_done(4)
+    hidden_pass(0, 0)
+    hidden_pass(0, 2)
     hidden_pass(0, 1)
-    hidden_pass(0, 0)
+    x_up(7)
     x_down(7)
-    x_up(7)
     mate_done(3, 2)
     hidden_pass(0, 3)
-    hidden_pass(0, 2)
     weight_pass(0, a, 1 - xh)
+    far_send(1)
+    far_send(0)
+    weight_pass(0, 1 - a, xh)
+    x_done(0)
+    weight_pass(0, 1 - a, 1 - xh)
+    near_send(0)
+    far_send(3)
+    near_send(1)
+    x_done(6)
     far_send(2)
-    far_send(0)
-    weight_pass(0, 1 - a, 1 - xh)
-    far_send(1)
-    x_done(6)
-    x_done(0)
     x_done(1)
-    weight_pass(0, 1 - a, xh)
-    near_send(0)
     x_done(7)
+    hidden_pass(1, 3)
+    dx_mate(1)
+    hidden_pass(1, 0)
     hidden_pass(1, 1)
-    far_send(3)
-    hidden_pass(1, 0)
-    x_pass(2)
-    near_send(1)
+    x_pass(0)
     hidden_pass(1, 2)
-    x_pass(0)
-    hidden_pass(1, 3)
     weight_pass(1, a, 1 - xh)
+    far_send(4)
     weight_pass(1, 1 - a, xh)
-    twin_send(5)
-    own_send()
-    far_send(4)
-    weight_pass(1, 1 - a, 1 - xh)
-    dx_mate(1)
     twin_send(6)
     x_pass(1)
+    near_send(2)
+    own_send()
+    dx_own(0)
+    x_pass(2)
+    weight_pass(0, a, xh)
+    weight_pass(1, 1 - a, 1 - xh)
+    x_sum(0)
+    dx_own(1)
+    z_far_4()
+    twin_send(5)
+    near_send(3)
     dx_mate(0)
-    near_send(2)
     x_pass(3)
-    dx_own(1)
-    weight_pass(0, a, xh)
-    x_sum(0)
     near_send(4)
-    dx_own(0)
-    z_far_4()
+    dx_pair(1)
+    dx_send(2, 3)
+    twin_pass(6)
+    weight_pass(1, a, xh)
+    x_sum(1)
+    z_far_up()
+    x_pass(4)
+    twin_send(7)
+    x_sum(2)
+    z_far_down()
+    twin_pass(5)
+    own_total()
+    full_sum(6)
+    x_sum(3)
+    z_near(3)
     dx_pair(0)
     dx_send(1)
-    dx_pair(1)
-    dx_send(2, 3)
-    twin_pass(5)
-    weight_pass(1, a, xh)
-    near_send(3)
-    twin_pass(6)
-    x_pass(4)
-    x_sum(1)
-    z_far_up()
-    x_sum(2)
-    z_far_down()
-    twin_send(7)
-    own_total()
-    full_sum(5)
-    full_sum(6)
-    x_sum(3)
     x_sum(4)
-    z_near(3)
     z_near(4)
     twin_pass(7)
+    full_sum(5)
     full_sum(7)
     total_send()
     dx_done()

time: 62.3 us -> 61.8 us (level)
  no operation moved by 1% of the time
where the time goes in v8:
time: 61.8 us; the launch traced here: 61.7 us
  Pallas kernels  61.1 us (99%)
  between operations  0.64 us (1%)
    pallas_call x1, Pallas kernels, shards(): pl.pallas_call(kernel, out_shape=(jax.ShapeDtypeStruct((128, 1024), BF16)...  59.3 us
    pallas_call x1, Pallas kernels, shards(): pl.pallas_call(finish, out_shape=(jax.ShapeDtypeStruct((128, 1024), BF16)...  1.79 us

profile of v8, /device:TPU:2, one launch (start us, length us, event | category | flops | bytes accessed | tf_op | source)
XLA Modules:
  0.0 61.7 jit_solution(15213192393614317159)
XLA Ops:
  0.6 59.3 %mlp_backward.1 = (bf16[128,1024]{1,0:T(8,128)(2,1)}, bf16[2,2,256,128]{3,2,1,0:T(8,128)(2,1)}) custom-call(bf16[128,1024]{1,0:T(8,128)(2,1)} %tok.1, bf16[128,1024]{1,0:T(8,128)(2,1)} %dy.1, bf16[128,256]{1,0:T(8,128)(2,1)} %wu.1, bf16[256,128]{1,0:T(8,128)(2,1)} %wd.1), custom_call_target="tpu_custom_call" | custom-call | flops 5368709120 | bytes 2097152 | tf_op jit(solution)/shard_map/mlp_backward/pallas_call | solution.py:498
  59.9 1.8 %finish.1 = (bf16[128,1024]{1,0:T(8,128)(2,1)}, bf16[128,256]{1,0:T(8,128)(2,1)}, bf16[256,128]{1,0:T(8,128)(2,1)}) custom-call(bf16[128,1024]{1,0:T(8,128)(2,1)} %get-tuple-element.5.dx, bf16[2,2,256,128]{3,2,1,0:T(8,128)(2,1)} %get-tuple-element.6.gw), custom_call_target="tpu_custom_call" | custom-call | tf_op jit(solution)/shard_map/finish/pallas_call | solution.py:548
